TPU v7x, 256 devices: a whole 4x4x8 slice. The times are simulated.
256 devices in a mesh: lon: 64 (over z, y, x_hi), spc: 4 (over x_lo, core).
Axes of the slice: x: 4 (x_hi: 2, x_lo: 2; x = x_hi * 2 + x_lo), y: 4, z: 8, core: 2. Of those that a mesh axis runs over, the one named last changes fastest.
Arguments:
- compound_group_loads: float32 [40, 9, 4, 1024, 128], P('spc', None, None, 'lon'), may hold values from 0.01 to 1
- leftover_stepfrac: float32 [4, 1024, 128], P('spc', 'lon'), may hold values from 0 to 1
- thermal_kelvins: float32 [4, 1024, 128], P('spc', 'lon'), may hold values from 250 to 310
- diffusive_numbers: float32 [3, 1024, 128], P(None, 'lon'), may hold values from 0.1 to 10
- whole_shifts: int32 [128], replicated, may hold values from 0 to 31, as said below
Outputs:
- particle: float32 [40, 9, 4, 1024, 128], P('spc', None, None, 'lon')
- zonal_flux: float32 [40, 4, 1024, 128], P('spc', None, 'lon')
Inputs may be any that keep to these rules, and one draw needn't show every extreme that they name: `whole_shifts`: rows 32 and beyond have offsets of at most 15. Row 0 takes 31 and row 32 takes 16 - 1.
All inputs are finite; a program needn't handle non-finite values.
Results may differ from a plain program's by a relative error of at most 0.0001.
Values sent between devices are 32-bit elements; how exact they have to be, the bound alone decides.
No kernel may reach another device: no remote copies, remote signals or barrier semaphores. Data moves between devices by JAX's collectives and lax.ppermute only.
A program may use at most 64 MiB of HBM per device.

v0:
```python
import functools

import jax
import jax.numpy as jnp
from jax import lax
from jax.experimental import pallas as pl
from jax.experimental.pallas import tpu as pltpu
from jax.sharding import PartitionSpec as P

BINS = 9
LEVELS = 4
PITERS = 2
CELLS = 16
ROWS = 128
POLAR = 32
SEED = 1.0
HEAT_OF_BOILING = 5000.0
CHUNKS = (2, 3, 3, 2)
SPARES = ((1, 0), (2, 0), (8, 8))

VMEM = pltpu.VMEM
COST = pl.CostEstimate(flops=1, bytes_accessed=1, transcendentals=0)
PARAMS = pltpu.CompilerParams(vmem_limit_bytes=16 * 2**20)
f32, i32 = jnp.float32, jnp.int32


def from_behind(block, axis, distance):
    devices = range(lax.axis_size(axis))
    route = [((i - distance) % len(devices), i) for i in devices]
    return lax.ppermute(block, axis, route)


def swapped(block, mask):
    route = [(i, i ^ mask) for i in range(lax.axis_size("spc"))]
    return lax.ppermute(block, "spc", route)


def any_specs(count):
    return [pl.BlockSpec(memory_space=pl.ANY)] * count


def along_lanes(values, index):
    return jnp.take_along_axis(values, index, axis=1, mode="promise_in_bounds")


def along_cells(values, index):
    return jnp.take_along_axis(values, index, axis=0, mode="promise_in_bounds")


def vreg_iota(dim):
    return lax.broadcasted_iota(i32, (8, ROWS), dim)


def padded(rows):
    return -(-rows // 8) * 8


def packing(needed):
    ones = jnp.where(needed, 1.0, 0.0).astype(jnp.bfloat16)
    row = lax.broadcasted_iota(i32, (ROWS, ROWS), 0)
    lane = lax.broadcasted_iota(i32, (ROWS, ROWS), 1)
    upto = jnp.where(row <= lane, 1.0, 0.0).astype(jnp.bfloat16)
    ranked = jnp.dot(ones, upto, preferred_element_type=f32).astype(i32)
    count = jnp.sum(jnp.where(needed, 1, 0), axis=1, keepdims=True)
    offsets, running = [], jnp.zeros((1, 1), i32)
    for cell in range(CELLS):
        offsets.append(running)
        running = running + count[cell : cell + 1]
    ends = offsets[1:] + [running]
    offset = jnp.concatenate(offsets, axis=0)
    lanes = lax.broadcasted_iota(i32, (CELLS, ROWS), 1)
    heights = lax.broadcasted_iota(i32, (CELLS, ROWS), 0)
    flat = offset + ranked - 1
    unpack_lane = flat & 127
    unpack_row = (offset >> 7) + jnp.where(lanes < (offset & 127), 1, 0)
    place = heights * ROWS + lanes
    pack_row = jnp.zeros((CELLS, ROWS), i32)
    for cell in range(CELLS):
        pack_row = pack_row + jnp.where(place >= ends[cell], 1, 0)
    pack_row = jnp.minimum(pack_row, CELLS - 1)
    wanted = (lanes - offset) & 127
    halves = []
    for half in range(2):
        at = slice(8 * half, 8 * half + 8)
        position = jnp.zeros((8, ROWS), i32)
        for step in (64, 32, 16, 8, 4, 2, 1):
            probe = along_lanes(ranked[at], position + (step - 1))
            position = jnp.where(probe <= wanted[at], position + step, position)
        halves.append(position)
    return (jnp.concatenate(halves, axis=0), pack_row, unpack_row, unpack_lane), running


def tables_kernel(shifts_ref, near_ref, polar_ref, which_ref):
    shifts = jnp.broadcast_to(shifts_ref[...], (CELLS, ROWS))
    cell = lax.broadcasted_iota(i32, (CELLS, ROWS), 0)
    needed = jnp.where(
        shifts < CELLS, jnp.where(cell <= shifts, 1, 0),
        jnp.where((cell == 0) | (cell > shifts - CELLS), 1, 0),
    ) > 0
    made, near_cells = packing(needed)
    for at, table in enumerate(made):
        near_ref[CELLS * at : CELLS * at + CELLS, :] = table
    within = vreg_iota(1) & (POLAR - 1)
    folded = along_lanes(shifts[:8], within)
    folded = jnp.concatenate([folded, folded], axis=0)
    needed = cell <= folded - CELLS
    (pack_lane, pack_row, unpack_row, unpack_lane), polar_cells = packing(needed)
    near_cells, polar_cells = jnp.sum(near_cells), jnp.sum(polar_cells)
    which_ref[0] = sum(
        jnp.where((near_cells > ROWS * (8 + a)) | (polar_cells > ROWS * (8 + c)), 1, 0)
        for a, c in SPARES[:-1]
    )
    polar_ref[0:16, :] = pack_lane
    polar_ref[16:32, :] = pack_row
    polar_ref[32:48, :] = unpack_row
    for level in range(LEVELS):
        for half in range(2):
            start = 48 + CELLS * level + 8 * half
            polar_ref[start : start + 8, :] = along_lanes(
                unpack_lane[8 * half : 8 * half + 8], within + POLAR * level
            )


def make_tables(shifts):
    return pl.pallas_call(
        tables_kernel,
        out_shape=(
            jax.ShapeDtypeStruct((4 * CELLS, ROWS), i32),
            jax.ShapeDtypeStruct((3 * CELLS + LEVELS * CELLS, ROWS), i32),
            jax.ShapeDtypeStruct((1,), i32),
        ),
        out_specs=(
            pl.BlockSpec(memory_space=VMEM),
            pl.BlockSpec(memory_space=VMEM),
            pl.BlockSpec(memory_space=pltpu.SMEM),
        ),
        name="tables",
        compiler_params=PARAMS,
    )(shifts)


def turning(shifts):
    back = vreg_iota(0) - shifts - 1
    return back & 7, (back & 15) >= 8


def turned(low, high, turn):
    index, swap = turn
    low, high = along_cells(low, index), along_cells(high, index)
    return jnp.where(swap, high, low), jnp.where(swap, low, high)


def far_masks(shifts):
    cell = vreg_iota(0)
    masks = []
    for half in range(2):
        at = cell + 8 * half
        polar = at <= shifts - CELLS
        behind = at <= shifts
        masks.append((behind, polar))
    return masks


def near_of(far, first):
    last = vreg_iota(0) == 7
    rolled = [pltpu.roll(half, 7, 0) for half in (far[0], far[1], first)]
    return (
        jnp.where(last, rolled[1], rolled[0]),
        jnp.where(last, rolled[2], rolled[1]),
    )


def table(ref, which, half):
    begin = CELLS * which + 8 * half
    return ref[begin : begin + 8, :]


def packer(table_ref, spare):
    lanes = (table(table_ref, 0, 0), table(table_ref, 0, 1))
    rows = table(table_ref, 1, 0)
    later = jnp.maximum(table(table_ref, 1, 1) - 8, 0)
    early, rows = rows < 8, rows & 7

    def pack_plane(low, high):
        low, high = along_lanes(low, lanes[0]), along_lanes(high, lanes[1])
        main = jnp.where(early, along_cells(low, rows), along_cells(high, rows))
        return main, along_cells(high, later) if spare else None

    return pack_plane


def folded_in(before, plane, place):
    if before is None:
        return list(plane)
    here = vreg_iota(1) >= POLAR * place
    return [
        jnp.where(here, pltpu.roll(half, POLAR * place, 1), old)
        for half, old in zip(plane, before)
    ]


def put_extra(ref, lead, begin, spare, extra):
    if spare == 8:
        ref[(*lead, pl.ds(pl.multiple_of(begin, 8), 8), slice(None))] = extra
    else:
        for row in range(spare):
            ref[(*lead, pl.ds(begin + row, 1), slice(None))] = extra[row : row + 1]


def get_extra(ref, lead, begin, spare):
    if spare == 8:
        return [ref[(*lead, pl.ds(pl.multiple_of(begin, 8), 8), slice(None))]]
    return [
        jnp.broadcast_to(ref[(*lead, pl.ds(begin + row, 1), slice(None))], (8, ROWS))
        for row in range(spare)
    ]


def liner(table_ref, spare):
    row0, row1 = table(table_ref, 2, 0) & 7, table(table_ref, 2, 1)
    low_row, late_row = row1 & 7, row1 >= 8

    def lines(main, extra):
        low, high = along_cells(main, row0), along_cells(main, low_row)
        if spare == 8:
            high = jnp.where(late_row, along_cells(extra[0], low_row), high)
        else:
            for row, late in enumerate(extra):
                high = jnp.where(row1 == 8 + row, late, high)
        return [low, high]

    return lines


def far_of(own, behind, beyond, masks):
    return [
        jnp.where(masks[h][1], beyond[h], jnp.where(masks[h][0], behind[h], own[h]))
        for h in range(2)
    ]


def species_kernel(me_ref, shifts_ref, loads_ref, after_ref, keep_ref, send_ref):
    del after_ref
    shifts = jnp.broadcast_to(shifts_ref[...], (8, ROWS))
    turn = turning(shifts)
    species = loads_ref.shape[0]

    def body(b, carry):
        for away, (part, at) in enumerate(((keep_ref, 0), (send_ref, 0), (keep_ref, 1), (send_ref, 1))):
            level = jnp.bitwise_xor(me_ref[0], away)
            low = sum(loads_ref[s, b, level, 0:8, :] for s in range(1, species))
            high = sum(loads_ref[s, b, level, 8:16, :] for s in range(1, species))
            low = low + loads_ref[0, b, level, 0:8, :]
            high = high + loads_ref[0, b, level, 8:16, :]
            low, high = turned(low, high, turn)
            part[at, b, 0:8, :] = low
            part[at, b, 8:16, :] = high
        return carry

    lax.fori_loop(0, BINS, body, 0)


def species_sums(me, shifts, loads, after):
    return pl.pallas_call(
        species_kernel,
        out_shape=(jax.ShapeDtypeStruct((2, BINS, CELLS, ROWS), f32),) * 2,
        in_specs=[
            pl.BlockSpec(memory_space=pltpu.SMEM),
            pl.BlockSpec(memory_space=VMEM),
            pl.BlockSpec(memory_space=VMEM),
        ]
        + any_specs(1),
        out_specs=(pl.BlockSpec(memory_space=VMEM),) * 2,
        name="species_sums",
        compiler_params=PARAMS,
        cost_estimate=COST,
    )(me, shifts, loads, after)


PLANES = 2 * BINS
SUMS = PLANES * CELLS
FOLDS = -(-PLANES // LEVELS)


def chip_kernel(keep_ref, got_ref, frac_ref, east_ref, temp_ref, out_ref):
    for at in range(2):
        for b in range(BINS):
            begin = CELLS * (BINS * at + b)
            out_ref[begin : begin + CELLS, :] = keep_ref[at, b] + got_ref[at, b]
    frac = (frac_ref[0, 0:8, :], frac_ref[0, 8:16, :])
    east = near_of(frac, jnp.broadcast_to(east_ref[0], (8, ROWS)))
    for half in range(2):
        begin = SUMS + 8 * half
        out_ref[begin : begin + 8, :] = 1.0 - east[half]
        out_ref[begin + 16 : begin + 24, :] = frac[half]
        out_ref[begin + 32 : begin + 40, :] = temp_ref[0, 8 * half : 8 * half + 8, :]


def chip_sums(keep, got, frac, east, temp):
    return pl.pallas_call(
        chip_kernel,
        out_shape=jax.ShapeDtypeStruct((SUMS + 3 * CELLS, ROWS), f32),
        in_specs=[pl.BlockSpec(memory_space=VMEM)] * 5,
        out_specs=pl.BlockSpec(memory_space=VMEM),
        name="chip_sums",
        compiler_params=PARAMS,
        cost_estimate=COST,
    )(keep, got, frac, east, temp)


def all_kernel(spare, polar_spare, near_ref, polar_ref, mine_ref, other_ref, own_ref, ahead_ref, beyond_ref):
    pack_near, pack_polar = packer(near_ref, spare), packer(polar_ref, polar_spare)
    folded = None
    for plane in range(PLANES):
        begin = CELLS * plane
        across = CELLS * ((plane + BINS) % PLANES)
        low = mine_ref[begin : begin + 8, :] + other_ref[across : across + 8, :]
        high = mine_ref[begin + 8 : begin + 16, :] + other_ref[across + 8 : across + 16, :]
        own_ref[begin : begin + 8, :] = low
        own_ref[begin + 8 : begin + 16, :] = high
        main, extra = pack_near(low, high)
        ahead_ref[8 * plane : 8 * plane + 8, :] = main
        put_extra(ahead_ref, (), 8 * PLANES + plane * spare, spare, extra)
        place = plane % LEVELS
        folded = folded_in(folded if place else None, (low, high), place)
        if place == LEVELS - 1 or plane == PLANES - 1:
            fold = plane // LEVELS
            main, extra = pack_polar(*folded)
            beyond_ref[8 * fold : 8 * fold + 8, :] = main
            put_extra(beyond_ref, (), 8 * FOLDS + fold * polar_spare, polar_spare, extra)


def all_sums(spares, near_table, polar_table, mine, other):
    spare, polar_spare = spares
    return pl.pallas_call(
        functools.partial(all_kernel, spare, polar_spare),
        out_shape=(
            jax.ShapeDtypeStruct((SUMS, ROWS), f32),
            jax.ShapeDtypeStruct((padded((8 + spare) * PLANES), ROWS), f32),
            jax.ShapeDtypeStruct(((8 + polar_spare) * FOLDS, ROWS), f32),
        ),
        in_specs=[pl.BlockSpec(memory_space=VMEM)] * 4,
        out_specs=(pl.BlockSpec(memory_space=VMEM),) * 3,
        name="all_sums",
        compiler_params=PARAMS,
        cost_estimate=COST,
    )(near_table, polar_table, mine, other)


def organic_kernel(
    spare, polar_spare,
    shifts_ref, near_ref, polar_ref, own_ref, behind_ref, beyond_ref, mine_ref, other_ref, after_ref,
    out_ref,
):
    del after_ref
    shifts = jnp.broadcast_to(shifts_ref[...], (8, ROWS))
    masks = far_masks(shifts)
    is_polar = shifts >= CELLS
    near_lines, polar_lines = liner(near_ref, spare), liner(polar_ref, polar_spare)
    lanes = (table(near_ref, 3, 0), table(near_ref, 3, 1))
    spread = None
    for at, meta_ref in enumerate((mine_ref, other_ref)):
        meta = [
            [meta_ref[SUMS + 16 * n + 8 * h : SUMS + 16 * n + 8 * h + 8, :] for h in range(2)]
            for n in range(3)
        ]
        rest, frac, temp = meta
        advected = []
        for b in range(BINS):
            plane = BINS * at + b
            begin, fold, place = CELLS * plane, plane // LEVELS, plane % LEVELS
            own = (own_ref[begin : begin + 8, :], own_ref[begin + 8 : begin + 16, :])
            if place == 0:
                spread = polar_lines(
                    beyond_ref[8 * fold : 8 * fold + 8, :],
                    get_extra(beyond_ref, (), 8 * FOLDS + fold * polar_spare, polar_spare),
                )
            lines = near_lines(
                behind_ref[8 * plane : 8 * plane + 8, :],
                get_extra(behind_ref, (), 8 * PLANES + plane * spare, spare),
            )
            behind = [along_lanes(lines[h], lanes[h]) for h in range(2)]
            beyond = [along_lanes(spread[h], table(polar_ref, 3 + place, h)) for h in range(2)]
            far = far_of(own, behind, beyond, masks)
            near = near_of(far, jnp.where(is_polar, behind[0], own[0]))
            advected.append([rest[h] * near[h] + frac[h] * far[h] for h in range(2)])
        for half in range(2):
            base = (298.15 / temp[half]) * jnp.exp(
                HEAT_OF_BOILING * (1.0 / 298.15 - 1.0 / temp[half])
            )
            organic = SEED + sum(advected[b][half] for b in range(BINS))
            for _ in range(PITERS):
                ratio = base / organic
                organic = SEED + sum(
                    advected[b][half] / (1.0 + 10.0 ** (b - 3) * ratio) for b in range(BINS)
                )
            out_ref[at, 8 * half : 8 * half + 8, :] = rest[half]
            out_ref[at, 16 + 8 * half : 24 + 8 * half, :] = frac[half]
            out_ref[at, 32 + 8 * half : 40 + 8 * half, :] = base / organic


def organic_of(spares, shifts, near_table, polar_table, own, behind, beyond, mine, other, after):
    return pl.pallas_call(
        functools.partial(organic_kernel, *spares),
        out_shape=jax.ShapeDtypeStruct((2, 3 * CELLS, ROWS), f32),
        in_specs=[pl.BlockSpec(memory_space=VMEM)] * 8 + any_specs(1),
        out_specs=pl.BlockSpec(memory_space=VMEM),
        name="organic",
        compiler_params=PARAMS,
        cost_estimate=COST,
    )(shifts, near_table, polar_table, own, behind, beyond, mine, other, after)


def pack_kernel(
    spare, polar_spare, start, shifts_ref, near_ref, polar_ref, loads_ref, *rest
):
    ahead_ref, beyond_ref = rest[-2:]
    shifts = jnp.broadcast_to(shifts_ref[...], (8, ROWS))
    turn = turning(shifts)
    s = pl.program_id(0) + start

    pack_near, pack_polar = packer(near_ref, spare), packer(polar_ref, polar_spare)

    def body(b, totals):
        folded, sums = None, []
        for level in range(LEVELS):
            low, high = turned(
                loads_ref[s, b, level, 0:8, :], loads_ref[s, b, level, 8:16, :], turn
            )
            sums.append(totals[level] + (low + high))
            folded = folded_in(folded, (low, high), level)
            main, extra = pack_near(low, high)
            plane = b * LEVELS + level
            ahead_ref[0, pl.ds(pl.multiple_of(8 * plane, 8), 8), :] = main
            put_extra(ahead_ref, (0,), 8 * BINS * LEVELS + plane * spare, spare, extra)
        main, extra = pack_polar(*folded)
        beyond_ref[0, pl.ds(pl.multiple_of(8 * b, 8), 8), :] = main
        put_extra(beyond_ref, (0,), 8 * BINS + b * polar_spare, polar_spare, extra)
        return tuple(sums)

    totals = lax.fori_loop(0, BINS, body, (jnp.zeros((8, ROWS), f32),) * LEVELS, unroll=3)
    begin = (8 + spare) * BINS * LEVELS
    for level in range(LEVELS):
        ahead_ref[0, begin + level : begin + level + 1, :] = jnp.sum(
            totals[level], axis=0, keepdims=True
        )


def packed_rows(spare, polar_spare):
    return (
        padded((8 + spare) * BINS * LEVELS + LEVELS),
        (8 + polar_spare) * BINS,
    )


def whole_spec(shape):
    return pl.BlockSpec(shape, lambda i: (0,) * len(shape))


def pack(spares, start, count, shifts, near_table, polar_table, loads, after, before):
    rows, polar_rows = packed_rows(*spares)
    species = loads.shape[0]
    args = [shifts, near_table, polar_table, loads, *after]
    in_specs = [pl.BlockSpec(memory_space=VMEM)] * 4 + any_specs(len(after))
    aliases = {}
    if before is not None:
        aliases = {len(args): 1}
        args.append(before)
        in_specs.append(pl.BlockSpec(memory_space=pl.ANY))
    return pl.pallas_call(
        functools.partial(pack_kernel, *spares, start),
        grid=(count,),
        out_shape=(
            jax.ShapeDtypeStruct((count, rows, ROWS), f32),
            jax.ShapeDtypeStruct((species, polar_rows, ROWS), f32),
        ),
        in_specs=in_specs,
        out_specs=(
            pl.BlockSpec((1, rows, ROWS), lambda i: (i, 0, 0)),
            pl.BlockSpec((1, polar_rows, ROWS), lambda i: (i + start, 0, 0)),
        ),
        input_output_aliases=aliases,
        name=f"pack_{start}",
        compiler_params=PARAMS,
        cost_estimate=COST,
    )(*args)


def weights_kernel(me_ref, pair_ref, other_ref, diff_ref, near_w, far_w, solve, fracs):
    for half in range(2):
        at = slice(8 * half, 8 * half + 8)
        diffusive = [diff_ref[k, at, :] for k in range(LEVELS - 1)]
        nothing = jnp.zeros((8, ROWS), f32)
        lower = [nothing] + diffusive
        upper = diffusive + [nothing]
        previous = nothing
        for k in range(LEVELS):
            pivot = 1.0 + lower[k] + upper[k] - lower[k] * previous
            inverse = 1.0 / pivot
            previous = upper[k] * inverse
            solve[0, k, at, :] = inverse
            solve[1, k, at, :] = lower[k] * inverse
            solve[2, k, at, :] = previous
    for away in range(LEVELS):
        level_ref = (pair_ref, other_ref)[away & 1].at[away >> 1]
        level = jnp.bitwise_xor(me_ref[0], away)
        for half in range(2):
            at = slice(8 * half, 8 * half + 8)
            rest_of = level_ref[8 * half : 8 * half + 8, :]
            frac = level_ref[16 + 8 * half : 24 + 8 * half, :]
            ratio = level_ref[32 + 8 * half : 40 + 8 * half, :]
            fracs[level, at, :] = frac
            inverse = solve[0, level, at, :]
            near_top, far_top = rest_of * inverse, frac * inverse
            for b in range(BINS):
                weight = 1.0 / (1.0 + 10.0 ** (b - 3) * ratio)
                near_w[b, level, at, :] = near_top * weight
                far_w[b, level, at, :] = far_top * weight


def weights_of(me, pair, other, diffusive):
    block = (LEVELS, CELLS, ROWS)
    return pl.pallas_call(
        weights_kernel,
        out_shape=tuple(
            jax.ShapeDtypeStruct(shape, f32)
            for shape in ((BINS,) + block, (BINS,) + block, (3,) + block, block)
        ),
        in_specs=[pl.BlockSpec(memory_space=pltpu.SMEM)] + [pl.BlockSpec(memory_space=VMEM)] * 3,
        out_specs=(pl.BlockSpec(memory_space=VMEM),) * 4,
        name="weights",
        compiler_params=PARAMS,
        cost_estimate=COST,
    )(me, pair, other, diffusive)


def final_kernel(
    spare, polar_spare, start,
    shifts_ref, near_ref, polar_ref, near_w, far_w, solve, fracs, loads_ref, behind_ref, beyond_ref,
    *rest,
):
    particle_ref, flux_ref = rest[-2:]
    shifts = jnp.broadcast_to(shifts_ref[...], (8, ROWS))
    halves = (slice(0, 8), slice(8, 16))
    turn = turning(shifts)
    masks = far_masks(shifts)
    is_polar = shifts >= CELLS
    i = pl.program_id(0)
    s = i + start

    near_lines, polar_lines = liner(near_ref, spare), liner(polar_ref, polar_spare)
    lanes = (table(near_ref, 3, 0), table(near_ref, 3, 1))

    def body(b, carry):
        spread = polar_lines(
            beyond_ref[s, pl.ds(pl.multiple_of(8 * b, 8), 8), :],
            get_extra(beyond_ref, (s,), 8 * BINS + b * polar_spare, polar_spare),
        )
        forward = [None] * LEVELS
        previous = None
        sums = []
        for k in range(LEVELS):
            low, high = loads_ref[s, b, k, 0:8, :], loads_ref[s, b, k, 8:16, :]
            own = turned(low, high, turn)
            plane = b * LEVELS + k
            lines = near_lines(
                behind_ref[i, pl.ds(pl.multiple_of(8 * plane, 8), 8), :],
                get_extra(behind_ref, (i,), 8 * BINS * LEVELS + plane * spare, spare),
            )
            behind = [along_lanes(lines[h], lanes[h]) for h in range(2)]
            beyond = [along_lanes(spread[h], table(polar_ref, 3 + k, h)) for h in range(2)]
            far = far_of(own, behind, beyond, masks)
            first = jnp.where(is_polar, behind[0], own[0])
            near = near_of(far, first)
            terms = (far[0], far[1], first, low, high)
            sums.append(tuple(a + t for a, t in zip(carry[k], terms)))
            step = []
            for half, at in enumerate(halves):
                value = near_w[b, k, at, :] * near[half] + far_w[b, k, at, :] * far[half]
                if k:
                    value = value + solve[1, k, at, :] * previous[half]
                step.append(value)
            forward[k] = previous = step
        following = forward[LEVELS - 1]
        for half, at in enumerate(halves):
            particle_ref[0, b, LEVELS - 1, at, :] = following[half]
        for k in range(LEVELS - 2, -1, -1):
            following = [
                forward[k][half] + solve[2, k, at, :] * following[half]
                for half, at in enumerate(halves)
            ]
            for half, at in enumerate(halves):
                particle_ref[0, b, k, at, :] = following[half]
        return tuple(sums)

    zero = jnp.zeros((8, ROWS), f32)
    sums = lax.fori_loop(0, BINS, body, ((zero,) * 5,) * LEVELS, unroll=3)
    cell = vreg_iota(0)
    within = shifts & (CELLS - 1)
    for k in range(LEVELS):
        far0, far1, first, low, high = sums[k]
        near0, near1 = near_of((far0, far1), first)
        counted = jnp.where((cell >= 1) & (cell <= within), far0, 0.0) + jnp.where(
            cell + 8 <= within, far1, 0.0
        )
        window = jnp.sum(counted, axis=0, keepdims=True)
        begin = (8 + spare) * BINS * LEVELS + k
        window = window + jnp.where(
            shifts_ref[...] >= CELLS, behind_ref[i, begin : begin + 1, :], 0.0
        )
        base = jnp.broadcast_to(window, (8, ROWS))
        for half, (gained, lost, far) in enumerate(((low, near0, far0), (high, near1, far1))):
            change = gained - lost
            running = change
            for step in (1, 2, 4):
                running = running + jnp.where(cell >= step, pltpu.roll(running, step, 0), 0.0)
            at = halves[half]
            flux_ref[0, k, at, :] = base + (running - change) + fracs[k, at, :] * far
            if half == 0:
                base = base + jnp.broadcast_to(running[7:8, :], (8, ROWS))


def final(
    spares, start, count, shifts, near_table, polar_table, weights, loads, behind, beyond, before
):
    species = loads.shape[0]
    outs = (
        jax.ShapeDtypeStruct((species, BINS, LEVELS, CELLS, ROWS), f32),
        jax.ShapeDtypeStruct((species, LEVELS, CELLS, ROWS), f32),
    )
    args = [shifts, near_table, polar_table, *weights, loads, behind, beyond]
    in_specs = [pl.BlockSpec(memory_space=VMEM)] * len(args)
    aliases = {}
    if before is not None:
        aliases = {len(args): 0, len(args) + 1: 1}
        args += list(before)
        in_specs += [pl.BlockSpec(memory_space=pl.ANY)] * 2
    return pl.pallas_call(
        functools.partial(final_kernel, *spares, start),
        grid=(count,),
        out_shape=outs,
        in_specs=in_specs,
        out_specs=(
            pl.BlockSpec((1, BINS, LEVELS, CELLS, ROWS), lambda i: (i + start, 0, 0, 0, 0)),
            pl.BlockSpec((1, LEVELS, CELLS, ROWS), lambda i: (i + start, 0, 0, 0)),
        ),
        input_output_aliases=aliases,
        name=f"final_{start}",
        compiler_params=PARAMS,
        cost_estimate=COST,
    )(*args)


def along_meridian(block):
    size = lax.axis_size("lon")
    return lax.ppermute(block, "lon", [(i, (i + 2) % size) for i in range(1, size, 2)])


def crossed(block):
    return lax.ppermute(block, "lon", [(i, i ^ 1) for i in range(lax.axis_size("lon"))])


def pipeline(spares, me, shifts, near_table, polar_table, loads, frac, temp, diffusive):
    tables = (shifts, near_table, polar_table)
    odd = lax.axis_index("lon") % 2 == 1
    starts = [sum(CHUNKS[:i]) for i in range(len(CHUNKS))]
    last = len(CHUNKS) - 1
    east = from_behind(frac[:, :1, :], "lon", -1)
    keep, send = species_sums(me, shifts, loads, near_table)
    got = swapped(send, 1)
    mine = chip_sums(keep, got, frac, east, temp)
    other = swapped(mine, 2)
    own, ahead_sums, beyond_sums = all_sums(spares, near_table, polar_table, mine, other)
    after, beyond, aheads = [keep], None, [None] * len(CHUNKS)
    for at in (0, last, 2, 1):
        aheads[at], beyond = pack(
            spares, starts[at], CHUNKS[at], *tables, loads, after, beyond
        )
        after = [aheads[at], own] if at == 2 else [aheads[at]]
    relayed = along_meridian(aheads[last])
    aheads[0], _ = lax.optimization_barrier((aheads[0], mine))
    behind = [from_behind(aheads[0], "lon", 1), from_behind(aheads[1], "lon", 1)]
    sums_behind = from_behind(ahead_sums, "lon", 1)
    sums_beyond = from_behind(beyond_sums, "lon", 2)
    beyond = from_behind(beyond, "lon", 2)
    aheads[2], behind[0] = lax.optimization_barrier((aheads[2], behind[0]))
    behind.append(from_behind(aheads[2], "lon", 1))
    mixed, sums_behind, sums_beyond = lax.optimization_barrier(
        (jnp.where(odd, relayed, aheads[last]), sums_behind, sums_beyond)
    )
    behind.append(crossed(mixed))
    level = organic_of(spares, *tables, own, sums_behind, sums_beyond, mine, other, behind[0])
    weights = weights_of(me, level, swapped(level, 1), diffusive)
    outs = None
    for start, count, block in zip(starts, CHUNKS, behind):
        outs = final(spares, start, count, *tables, weights, loads, block, beyond, outs)
    return tuple(outs)


def per_device(loads, frac, temp, diffusive, whole_shifts):
    me = lax.axis_index("spc").astype(i32).reshape(1)
    shifts = whole_shifts.reshape(1, ROWS)
    near_table, polar_table, which = make_tables(shifts)
    branches = [functools.partial(pipeline, spares) for spares in SPARES]
    return lax.switch(
        which[0], branches, me, shifts, near_table, polar_table, loads, frac, temp, diffusive
    )


def solution(mesh):
    placed = (
        P("spc", None, None, "lon", None),
        P("spc", "lon", None),
        P("spc", "lon", None),
        P(None, "lon", None),
        P(),
    )
    return jax.shard_map(
        per_device,
        mesh=mesh,
        in_specs=placed,
        out_specs=(P("spc", None, None, "lon", None), P("spc", None, "lon", None)),
        check_vma=False,
    )
```

profile of v0, /device:TPU:1, one launch (start us, length us, event | category | flops | bytes accessed | tf_op | source)
XLA Modules:
  0.0 77.3 jit_solution(1067854056309386996)
XLA Ops:
  0.6 1.4 %tables.1 = (s32[64,128]{1,0:T(8,128)S(1)}, s32[112,128]{1,0:T(8,128)S(1)}, s32[1]{0:T(128)}) custom-call(s32[1,128]{1,0:T(1,128)} %bitcast.5), custom_call_target="tpu_custom_call" | custom-call | tf_op jit(solution)/shard_map/tables/pallas_call | solution.py:125
  2.7 74.6 %conditional.1 = ((f32[10,9,4,16,128]{4,3,2,1,0:T(8,128)}, f32[10,4,16,128]{3,2,1,0:T(8,128)})) conditional(s32[]{:T(128)} %bitcast.4, (s32[]{:T(128)}, s32[1,128]{1,0:T(1,128)}, f32[10,9,4,16,128]{4,3,2,1,0:T(8,128)}, s32[64,128]{1,0:T(8,128)S(1)}, f32[1,16,128]{2,1,0:T(8,128)}, /*index=5*/f32[1,16,128]{2,1,0:T(8,128)}, ...), branch_computations={%region_0.1_spmd, %region_1.2_spmd, %region_2.3_spmd} | conditional | flops 149532 | bytes 45545308 | solution.py:705
  2.7 0.0 copy-start.14
  2.7 0.0 copy-start
  2.7 0.0 copy-start.8
  2.7 0.0 copy-start.17
  2.7 2.3 %species_sums.3 = (f32[2,9,16,128]{3,2,1,0:T(8,128)S(1)}, f32[2,9,16,128]{3,2,1,0:T(8,128)S(1)}) custom-call(s32[1]{0:T(128)} %bitcast.me_ref, s32[1,128]{1,0:T(1,128)} %get-tuple-element.48.shifts_ref, f32[10,9,4,16,128]{4,3,2,1,0:T(8,128)} %get-tuple-element.190.loads_ref, s32[64,128]{1,0:T(8,128)S(1)} %get-tuple-element.49.after_ref.near_ref), custom_call_target="tpu_custom_call" | custom-call | flops 1 | bytes 1 | tf_op jit(solution)/shard_map/cond/branch_0_fun/species_sums/pallas_call | solution.py:264
  5.0 3.3 %collective-permute-start = (f32[2,9,16,128]{3,2,1,0:T(8,128)S(1)}, f32[2,9,16,128]{3,2,1,0:T(8,128)S(1)}, u32[]{:S(2)}, u32[]{:S(2)}) collective-permute-start(f32[2,9,16,128]{3,2,1,0:T(8,128)S(1)} %get-tuple-element.54), channel_id=1, source_target_pairs={{0,1},{1,0},{2,3},{3,2},{4,5},{5,4},{6,7},{7,6},{8,9},{9,8},{10,11... | collective-permute-start | bytes 442376 | tf_op jit(solution)/shard_map/cond/branch_0_fun/ppermute | solution.py:35
  8.4 0.0 copy-done.14
  8.4 8.8 %collective-permute-start.1 = (f32[1,1,128]{2,1,0:T(1,128)S(1)}, f32[1,1,128]{2,1,0:T(1,128)S(1)}, u32[]{:S(2)}, u32[]{:S(2)}) collective-permute-start(f32[1,1,128]{2,1,0:T(1,128)S(1)} %slice.6), channel_id=1, source_target_pairs={{4,0},{8,4},{12,8},{16,12},{20,16},{24,20},{28,24},{32,28},{36,32}... | collective-permute-start | bytes 1544 | tf_op jit(solution)/shard_map/cond/branch_0_fun/ppermute | solution.py:30
  17.1 0.0 copy-done
  17.1 0.0 copy-done.8
  17.2 1.0 %pack_0.3 = (f32[2,328,128]{2,1,0:T(8,128)S(1)}, f32[10,72,128]{2,1,0:T(8,128)S(1)}) custom-call(s32[1,128]{1,0:T(1,128)S(1)} %copy-done.8, s32[64,128]{1,0:T(8,128)S(1)} %get-tuple-element.49.after_ref.near_ref, s32[112,128]{1,0:T(8,128)S(1)} %get-tuple-element.50.polar_ref, f32[10,9,4,16,128]{4,3,2,1,0:T(8,128)S(1)} %copy-done, ...), custom_call_target="tpu_custom_call" | custom-call | flops 1 | bytes 1 | tf_op jit(solution)/shard_map/cond/branch_0_fun/pack_0/pallas_call | solution.py:470
  18.2 0.0 collective-permute-done.1.east_ref
  18.2 0.0 collective-permute-done.got_ref
  18.2 0.0 copy-done.17
  18.2 0.1 collective-permute-start.6
  18.3 1.0 %pack_8.3 = (f32[2,328,128]{2,1,0:T(8,128)S(1)}, f32[10,72,128]{2,1,0:T(8,128)S(1)}) custom-call(s32[1,128]{1,0:T(1,128)S(1)} %copy-done.8, s32[64,128]{1,0:T(8,128)S(1)} %get-tuple-element.49.after_ref.near_ref, s32[112,128]{1,0:T(8,128)S(1)} %get-tuple-element.50.polar_ref, f32[10,9,4,16,128]{4,3,2,1,0:T(8,128)S(1)} %copy-done, ...), custom_call_target="tpu_custom_call", output_to_operand_aliasing={{1}: (5, {})} | custom-call | flops 1 | bytes 1 | tf_op jit(solution)/shard_map/cond/branch_0_fun/pack_8/pallas_call | solution.py:470
  19.3 0.7 collective-permute-start.3
  20.0 0.4 collective-permute-start.2
  20.4 1.5 %pack_5.3 = (f32[3,328,128]{2,1,0:T(8,128)S(1)}, f32[10,72,128]{2,1,0:T(8,128)S(1)}) custom-call(s32[1,128]{1,0:T(1,128)S(1)} %copy-done.8, s32[64,128]{1,0:T(8,128)S(1)} %get-tuple-element.49.after_ref.near_ref, s32[112,128]{1,0:T(8,128)S(1)} %get-tuple-element.50.polar_ref, f32[10,9,4,16,128]{4,3,2,1,0:T(8,128)S(1)} %copy-done, ...), custom_call_target="tpu_custom_call", output_to_operand_aliasing={{1}: (5, {})} | custom-call | flops 1 | bytes 1 | tf_op jit(solution)/shard_map/cond/branch_0_fun/pack_5/pallas_call | solution.py:470
  22.0 8.0 %collective-permute-done.2.other_ref = f32[336,128]{1,0:T(8,128)S(1)} collective-permute-done((f32[336,128]{1,0:T(8,128)S(1)}, f32[336,128]{1,0:T(8,128)S(1)}, u32[]{:S(2)}, u32[]{:S(2)}) %collective-permute-start.2) | collective-permute-done | bytes 172064 | tf_op jit(solution)/shard_map/cond/branch_0_fun/ppermute | solution.py:35
  30.0 0.2 all_sums.3
  30.2 0.1 collective-permute-start.5
  30.3 0.1 collective-permute-start.4
  30.4 0.0 copy-start.11
  30.4 0.0 copy-start.1
  30.4 3.5 %pack_2.3 = (f32[3,328,128]{2,1,0:T(8,128)S(1)}, f32[10,72,128]{2,1,0:T(8,128)S(1)}) custom-call(s32[1,128]{1,0:T(1,128)S(1)} %copy-done.8, s32[64,128]{1,0:T(8,128)S(1)} %get-tuple-element.49.after_ref.near_ref, s32[112,128]{1,0:T(8,128)S(1)} %get-tuple-element.50.polar_ref, ...), custom_call_target="tpu_custom_call", output_to_operand_aliasing={{1}: (6, {})} | custom-call | flops 1 | bytes 1 | tf_op jit(solution)/shard_map/cond/branch_0_fun/pack_2/pallas_call | solution.py:470
  33.9 0.1 collective-permute-start.9
  34.0 0.0 collective-permute-done.6.after_ref.behind_ref
  34.0 3.2 %collective-permute-start.11 = (f32[3,328,128]{2,1,0:T(8,128)S(1)}, f32[3,328,128]{2,1,0:T(8,128)S(1)}, u32[]{:S(2)}, u32[]{:S(2)}) collective-permute-start(f32[3,328,128]{2,1,0:T(8,128)S(1)} %get-tuple-element.78), channel_id=1, source_target_pairs={{252,0},{0,4},{4,8},{8,12},{12,16},{16,20},{20,24},{24,28},{28,32}... | collective-permute-start | bytes 1511432 | tf_op jit(solution)/shard_map/cond/branch_0_fun/ppermute | solution.py:30
  37.3 0.0 collective-permute-done.3
  37.3 2.8 %collective-permute-start.10 = (f32[3,328,128]{2,1,0:T(8,128)S(1)}, f32[3,328,128]{2,1,0:T(8,128)S(1)}, u32[]{:S(2)}, u32[]{:S(2)}) collective-permute-start(f32[3,328,128]{2,1,0:T(8,128)S(1)} %get-tuple-element.77.rest_0_), channel_id=1, source_target_pairs={{252,0},{0,4},{4,8},{8,12},{12,16},{16,20},{20,24},{24,28},{28,32}... | collective-permute-start | bytes 1511432 | tf_op jit(solution)/shard_map/cond/branch_0_fun/ppermute | solution.py:30
  40.2 0.0 collective-permute-done.5.beyond_ref
  40.2 1.6 %collective-permute-done.4.behind_ref = f32[168,128]{1,0:T(8,128)S(1)} collective-permute-done((f32[168,128]{1,0:T(8,128)S(1)}, f32[168,128]{1,0:T(8,128)S(1)}, u32[]{:S(2)}, u32[]{:S(2)}) %collective-permute-start.4) | collective-permute-done | bytes 86048 | tf_op jit(solution)/shard_map/cond/branch_0_fun/ppermute | solution.py:30
  41.8 0.0 collective-permute-start.8
  41.8 0.3 organic.3.pair_ref
  42.2 3.1 %collective-permute-start.7 = (f32[2,48,128]{2,1,0:T(8,128)S(1)}, f32[2,48,128]{2,1,0:T(8,128)S(1)}, u32[]{:S(2)}, u32[]{:S(2)}) collective-permute-start(f32[2,48,128]{2,1,0:T(8,128)S(1)} %organic.3.pair_ref), channel_id=1, source_target_pairs={{0,1},{1,0},{2,3},{3,2},{4,5},{5,4},{6,7},{7,6},{8,9},{9,8},{10,11... | collective-permute-start | bytes 147464 | tf_op jit(solution)/shard_map/cond/branch_0_fun/ppermute | solution.py:35
  45.2 0.9 %collective-permute-done.7.other_ref = f32[2,48,128]{2,1,0:T(8,128)S(1)} collective-permute-done((f32[2,48,128]{2,1,0:T(8,128)S(1)}, f32[2,48,128]{2,1,0:T(8,128)S(1)}, u32[]{:S(2)}, u32[]{:S(2)}) %collective-permute-start.7) | collective-permute-done | bytes 49184 | tf_op jit(solution)/shard_map/cond/branch_0_fun/ppermute | solution.py:35
  46.1 0.1 weights.3
  46.2 10.8 %collective-permute-done.9.beyond_ref = f32[10,72,128]{2,1,0:T(8,128)S(1)} collective-permute-done((f32[10,72,128]{2,1,0:T(8,128)S(1)}, f32[10,72,128]{2,1,0:T(8,128)S(1)}, u32[]{:S(2)}, u32[]{:S(2)}) %collective-permute-start.9) | collective-permute-done | bytes 368672 | tf_op jit(solution)/shard_map/cond/branch_0_fun/ppermute | solution.py:30
  57.0 2.1 %final_0.3 = (f32[10,9,4,16,128]{4,3,2,1,0:T(8,128)}, f32[10,4,16,128]{3,2,1,0:T(8,128)}) custom-call(s32[1,128]{1,0:T(1,128)S(1)} %copy-done.8, s32[64,128]{1,0:T(8,128)S(1)} %get-tuple-element.49.after_ref.near_ref, s32[112,128]{1,0:T(8,128)S(1)} %get-tuple-element.50.polar_ref, f32[9,4,16,128]{3,2,1,0:T(8,128)S(1)} %get-tuple-element.70.near_w, ...), custom_call_target="tpu_custom_call" | custom-call | flops 1 | bytes 1 | tf_op jit(solution)/shard_map/cond/branch_0_fun/final_0/pallas_call | solution.py:638
  59.1 2.6 %collective-permute-done.11.behind_ref = f32[3,328,128]{2,1,0:T(8,128)S(1)} collective-permute-done((f32[3,328,128]{2,1,0:T(8,128)S(1)}, f32[3,328,128]{2,1,0:T(8,128)S(1)}, u32[]{:S(2)}, u32[]{:S(2)}) %collective-permute-start.11) | collective-permute-done | bytes 503840 | tf_op jit(solution)/shard_map/cond/branch_0_fun/ppermute | solution.py:30
  61.6 2.7 %final_2.3 = (f32[10,9,4,16,128]{4,3,2,1,0:T(8,128)}, f32[10,4,16,128]{3,2,1,0:T(8,128)}) custom-call(s32[1,128]{1,0:T(1,128)S(1)} %copy-done.8, s32[64,128]{1,0:T(8,128)S(1)} %get-tuple-element.49.after_ref.near_ref, s32[112,128]{1,0:T(8,128)S(1)} %get-tuple-element.50.polar_ref, ...), custom_call_target="tpu_custom_call", output_to_operand_aliasing={{0}: (10, {}), {1}: (11, {})} | custom-call | flops 1 | bytes 1 | tf_op jit(solution)/shard_map/cond/branch_0_fun/final_2/pallas_call | solution.py:638
  64.4 8.1 %collective-permute-done.10.behind_ref = f32[3,328,128]{2,1,0:T(8,128)S(1)} collective-permute-done((f32[3,328,128]{2,1,0:T(8,128)S(1)}, f32[3,328,128]{2,1,0:T(8,128)S(1)}, u32[]{:S(2)}, u32[]{:S(2)}) %collective-permute-start.10) | collective-permute-done | bytes 503840 | tf_op jit(solution)/shard_map/cond/branch_0_fun/ppermute | solution.py:30
  72.4 2.7 %final_5.3 = (f32[10,9,4,16,128]{4,3,2,1,0:T(8,128)}, f32[10,4,16,128]{3,2,1,0:T(8,128)}) custom-call(s32[1,128]{1,0:T(1,128)S(1)} %copy-done.8, s32[64,128]{1,0:T(8,128)S(1)} %get-tuple-element.49.after_ref.near_ref, s32[112,128]{1,0:T(8,128)S(1)} %get-tuple-element.50.polar_ref, ...), custom_call_target="tpu_custom_call", output_to_operand_aliasing={{0}: (10, {}), {1}: (11, {})} | custom-call | flops 1 | bytes 1 | tf_op jit(solution)/shard_map/cond/branch_0_fun/final_5/pallas_call | solution.py:638
  75.2 0.0 collective-permute-done.8.behind_ref
  75.2 2.1 %final_8.3 = (f32[10,9,4,16,128]{4,3,2,1,0:T(8,128)}, f32[10,4,16,128]{3,2,1,0:T(8,128)}) custom-call(s32[1,128]{1,0:T(1,128)S(1)} %copy-done.8, s32[64,128]{1,0:T(8,128)S(1)} %get-tuple-element.49.after_ref.near_ref, s32[112,128]{1,0:T(8,128)S(1)} %get-tuple-element.50.polar_ref, ...), custom_call_target="tpu_custom_call", output_to_operand_aliasing={{0}: (10, {}), {1}: (11, {})} | custom-call | flops 1 | bytes 1 | tf_op jit(solution)/shard_map/cond/branch_0_fun/final_8/pallas_call | solution.py:638
  (5 shorter events, 0.1 us)
Async XLA Ops:
  2.7 5.7 %copy-start.14 = (f32[1,16,128]{2,1,0:T(8,128)S(1)}, f32[1,16,128]{2,1,0:T(8,128)}, u32[]{:S(2)}) copy-start(f32[1,16,128]{2,1,0:T(8,128)} %get-tuple-element.193.frac_ref) | copy-start | bytes 24580 | tf_op jit(solution)/shard_map/cond
  2.7 14.4 %copy-start = (f32[10,9,4,16,128]{4,3,2,1,0:T(8,128)S(1)}, f32[10,9,4,16,128]{4,3,2,1,0:T(8,128)}, u32[]{:S(2)}) copy-start(f32[10,9,4,16,128]{4,3,2,1,0:T(8,128)} %get-tuple-element.190.loads_ref) | copy-start | bytes 8847364 | tf_op jit(solution)/shard_map/cond
  2.7 14.4 %copy-start.8 = (s32[1,128]{1,0:T(1,128)S(1)}, s32[1,128]{1,0:T(1,128)}, u32[]{:S(2)}) copy-start(s32[1,128]{1,0:T(1,128)} %get-tuple-element.48.shifts_ref) | copy-start | bytes 1540 | tf_op jit(solution)/shard_map/cond
  2.7 15.5 %copy-start.17 = (f32[1,16,128]{2,1,0:T(8,128)S(1)}, f32[1,16,128]{2,1,0:T(8,128)}, u32[]{:S(2)}) copy-start(f32[1,16,128]{2,1,0:T(8,128)} %get-tuple-element.196.temp_ref) | copy-start | bytes 24580 | tf_op jit(solution)/shard_map/cond
  5.0 13.1 %collective-permute-start = (f32[2,9,16,128]{3,2,1,0:T(8,128)S(1)}, f32[2,9,16,128]{3,2,1,0:T(8,128)S(1)}, u32[]{:S(2)}, u32[]{:S(2)}) collective-permute-start(f32[2,9,16,128]{3,2,1,0:T(8,128)S(1)} %get-tuple-element.54), channel_id=1, source_target_pairs={{0,1},{1,0},{2,3},{3,2},{4,5},{5,4},{6,7},{7,6},{8,9},{9,8},{10,11... | collective-permute-start | bytes 442376 | tf_op jit(solution)/shard_map/cond/branch_0_fun/ppermute | solution.py:35
  8.4 9.8 %collective-permute-start.1 = (f32[1,1,128]{2,1,0:T(1,128)S(1)}, f32[1,1,128]{2,1,0:T(1,128)S(1)}, u32[]{:S(2)}, u32[]{:S(2)}) collective-permute-start(f32[1,1,128]{2,1,0:T(1,128)S(1)} %slice.6), channel_id=1, source_target_pairs={{4,0},{8,4},{12,8},{16,12},{20,16},{24,20},{28,24},{32,28},{36,32}... | collective-permute-start | bytes 1544 | tf_op jit(solution)/shard_map/cond/branch_0_fun/ppermute | solution.py:30
  18.2 15.8 %collective-permute-start.6 = (f32[2,328,128]{2,1,0:T(8,128)S(1)}, f32[2,328,128]{2,1,0:T(8,128)S(1)}, u32[]{:S(2)}, u32[]{:S(2)}) collective-permute-start(f32[2,328,128]{2,1,0:T(8,128)S(1)} %get-tuple-element.67.rest_0_), channel_id=1, source_target_pairs={{252,0},{0,4},{4,8},{8,12},{12,16},{16,20},{20,24},{24,28},{28,32}... | collective-permute-start | bytes 1007624 | tf_op jit(solution)/shard_map/cond/branch_0_fun/ppermute | solution.py:30
  19.3 17.9 %collective-permute-start.3 = (f32[2,328,128]{2,1,0:T(8,128)S(1)}, f32[2,328,128]{2,1,0:T(8,128)S(1)}, u32[]{:S(2)}, u32[]{:S(2)}) collective-permute-start(f32[2,328,128]{2,1,0:T(8,128)S(1)} %get-tuple-element.60.rest_0_), channel_id=1, source_target_pairs={{4,12},{12,20},{20,28},{28,36},{36,44},{44,52},{52,60},{60,68},{68... | collective-permute-start | bytes 1007624 | tf_op jit(solution)/shard_map/cond/branch_0_fun/ppermute | solution.py:656
  20.0 10.0 %collective-permute-start.2 = (f32[336,128]{1,0:T(8,128)S(1)}, f32[336,128]{1,0:T(8,128)S(1)}, u32[]{:S(2)}, u32[]{:S(2)}) collective-permute-start(f32[336,128]{1,0:T(8,128)S(1)} %chip_sums.3.mine_ref), channel_id=1, source_target_pairs={{0,2},{1,3},{2,0},{3,1},{4,6},{5,7},{6,4},{7,5},{8,10},{9,11},{10,... | collective-permute-start | bytes 516104 | tf_op jit(solution)/shard_map/cond/branch_0_fun/ppermute | solution.py:35
  30.2 9.9 %collective-permute-start.5 = (f32[40,128]{1,0:T(8,128)S(1)}, f32[40,128]{1,0:T(8,128)S(1)}, u32[]{:S(2)}, u32[]{:S(2)}) collective-permute-start(f32[40,128]{1,0:T(8,128)S(1)} %get-tuple-element.62), channel_id=1, source_target_pairs={{248,0},{252,4},{0,8},{4,12},{8,16},{12,20},{16,24},{20,28},{24,32... | collective-permute-start | bytes 61448 | tf_op jit(solution)/shard_map/cond/branch_0_fun/ppermute | solution.py:30
  30.3 11.5 %collective-permute-start.4 = (f32[168,128]{1,0:T(8,128)S(1)}, f32[168,128]{1,0:T(8,128)S(1)}, u32[]{:S(2)}, u32[]{:S(2)}) collective-permute-start(f32[168,128]{1,0:T(8,128)S(1)} %get-tuple-element.61), channel_id=1, source_target_pairs={{252,0},{0,4},{4,8},{8,12},{12,16},{16,20},{20,24},{24,28},{28,32}... | collective-permute-start | bytes 258056 | tf_op jit(solution)/shard_map/cond/branch_0_fun/ppermute | solution.py:30
  30.4 15.7 %copy-start.11 = (f32[3,16,128]{2,1,0:T(8,128)S(1)}, f32[3,16,128]{2,1,0:T(8,128)}, u32[]{:S(2)}) copy-start(f32[3,16,128]{2,1,0:T(8,128)} %get-tuple-element.199.diff_ref) | copy-start | bytes 73732 | tf_op jit(solution)/shard_map/cond
  30.4 26.6 %copy-start.1 = (f32[10,9,4,16,128]{4,3,2,1,0:T(8,128)S(1)}, f32[10,9,4,16,128]{4,3,2,1,0:T(8,128)}, u32[]{:S(2)}) copy-start(f32[10,9,4,16,128]{4,3,2,1,0:T(8,128)} %get-tuple-element.190.loads_ref) | copy-start | bytes 8847364 | tf_op jit(solution)/shard_map/cond
  33.9 23.1 %collective-permute-start.9 = (f32[10,72,128]{2,1,0:T(8,128)S(1)}, f32[10,72,128]{2,1,0:T(8,128)S(1)}, u32[]{:S(2)}, u32[]{:S(2)}) collective-permute-start(f32[10,72,128]{2,1,0:T(8,128)S(1)} %get-tuple-element.76), channel_id=1, source_target_pairs={{248,0},{252,4},{0,8},{4,12},{8,16},{12,20},{16,24},{20,28},{24,32... | collective-permute-start | bytes 1105928 | tf_op jit(solution)/shard_map/cond/branch_0_fun/ppermute | solution.py:30
  34.0 27.6 %collective-permute-start.11 = (f32[3,328,128]{2,1,0:T(8,128)S(1)}, f32[3,328,128]{2,1,0:T(8,128)S(1)}, u32[]{:S(2)}, u32[]{:S(2)}) collective-permute-start(f32[3,328,128]{2,1,0:T(8,128)S(1)} %get-tuple-element.78), channel_id=1, source_target_pairs={{252,0},{0,4},{4,8},{8,12},{12,16},{16,20},{20,24},{24,28},{28,32}... | collective-permute-start | bytes 1511432 | tf_op jit(solution)/shard_map/cond/branch_0_fun/ppermute | solution.py:30
  37.3 35.2 %collective-permute-start.10 = (f32[3,328,128]{2,1,0:T(8,128)S(1)}, f32[3,328,128]{2,1,0:T(8,128)S(1)}, u32[]{:S(2)}, u32[]{:S(2)}) collective-permute-start(f32[3,328,128]{2,1,0:T(8,128)S(1)} %get-tuple-element.77.rest_0_), channel_id=1, source_target_pairs={{252,0},{0,4},{4,8},{8,12},{12,16},{16,20},{20,24},{24,28},{28,32}... | collective-permute-start | bytes 1511432 | tf_op jit(solution)/shard_map/cond/branch_0_fun/ppermute | solution.py:30
  41.8 33.3 %collective-permute-start.8 = (f32[2,328,128]{2,1,0:T(8,128)S(1)}, f32[2,328,128]{2,1,0:T(8,128)S(1)}, u32[]{:S(2)}, u32[]{:S(2)}) collective-permute-start(f32[2,328,128]{2,1,0:T(8,128)S(1)} %broadcast_select_fusion), channel_id=1, source_target_pairs={{0,4},{4,0},{8,12},{12,8},{16,20},{20,16},{24,28},{28,24},{32,36},... | collective-permute-start | bytes 1007624 | tf_op jit(solution)/shard_map/cond/branch_0_fun/ppermute | solution.py:660
  42.2 4.0 %collective-permute-start.7 = (f32[2,48,128]{2,1,0:T(8,128)S(1)}, f32[2,48,128]{2,1,0:T(8,128)S(1)}, u32[]{:S(2)}, u32[]{:S(2)}) collective-permute-start(f32[2,48,128]{2,1,0:T(8,128)S(1)} %organic.3.pair_ref), channel_id=1, source_target_pairs={{0,1},{1,0},{2,3},{3,2},{4,5},{5,4},{6,7},{7,6},{8,9},{9,8},{10,11... | collective-permute-start | bytes 147464 | tf_op jit(solution)/shard_map/cond/branch_0_fun/ppermute | solution.py:35
where the time goes:
time: 77.4 us; the launch traced here: 77.3 us
  waiting for transfers between devices  32 us (41%)
  starting transfers between devices  22.7 us (29%)
  Pallas kernels  21.1 us (27%)
  between operations  1.29 us (2%)
    ppermute x7, waiting for transfers between devices, from_behind(): return lax.ppermute(block, axis, route)  23 us
    ppermute x7, starting transfers between devices, from_behind(): return lax.ppermute(block, axis, route)  15.2 us
    pallas_call x4, Pallas kernels, final(): pl.pallas_call(functools.partial(final_kernel, *spares, start), grid=(cou...  9.63 us
    ppermute x3, waiting for transfers between devices, swapped(): return lax.ppermute(block, 'spc', route)  8.91 us
    pallas_call x4, Pallas kernels, pack(): pl.pallas_call(functools.partial(pack_kernel, *spares, start), grid=(coun...  7.07 us
    ppermute x3, starting transfers between devices, swapped(): return lax.ppermute(block, 'spc', route)  6.8 us
    pallas_call x1, Pallas kernels, species_sums(): pl.pallas_call(species_kernel, out_shape=(jax.ShapeDtypeStruct((2, BINS,...  2.28 us
  transfers between devices with their start and end apart: 12, of which 6 were waited for; matrix products, arithmetic and copies ran while one was open for 0% of the time, Pallas kernels for 20%

commit v1 on v0

--- a/solution.py
+++ b/solution.py
@@ -15,7 +15,7 @@
 POLAR = 32
 SEED = 1.0
 HEAT_OF_BOILING = 5000.0
-CHUNKS = (2, 3, 3, 2)
+CHUNKS = (2, 3, 2, 3)
 SPARES = ((1, 0), (2, 0), (8, 8))
 
 VMEM = pltpu.VMEM
@@ -676,24 +676,28 @@
         aheads[at], beyond = pack(
             spares, starts[at], CHUNKS[at], *tables, loads, after, beyond
         )
-        after = [aheads[at], own] if at == 2 else [aheads[at]]
+        after = [aheads[at]] + {0: [mine], 2: [own]}.get(at, [])
     relayed = along_meridian(aheads[last])
     aheads[0], _ = lax.optimization_barrier((aheads[0], mine))
     behind = [from_behind(aheads[0], "lon", 1), from_behind(aheads[1], "lon", 1)]
     sums_behind = from_behind(ahead_sums, "lon", 1)
     sums_beyond = from_behind(beyond_sums, "lon", 2)
     beyond = from_behind(beyond, "lon", 2)
-    aheads[2], behind[0] = lax.optimization_barrier((aheads[2], behind[0]))
+    aheads[2], aheads[1], behind[0] = lax.optimization_barrier(
+        (aheads[2], aheads[1], behind[0])
+    )
     behind.append(from_behind(aheads[2], "lon", 1))
-    mixed, sums_behind, sums_beyond = lax.optimization_barrier(
-        (jnp.where(odd, relayed, aheads[last]), sums_behind, sums_beyond)
+    mixed, _, sums_behind, sums_beyond = lax.optimization_barrier(
+        (jnp.where(odd, relayed, aheads[last]), aheads[1], sums_behind, sums_beyond)
     )
     behind.append(crossed(mixed))
     level = organic_of(spares, *tables, own, sums_behind, sums_beyond, mine, other, behind[0])
     weights = weights_of(me, level, swapped(level, 1), diffusive)
     outs = None
-    for start, count, block in zip(starts, CHUNKS, behind):
-        outs = final(spares, start, count, *tables, weights, loads, block, beyond, outs)
+    for at in (0, 1, last, 2):
+        outs = final(
+            spares, starts[at], CHUNKS[at], *tables, weights, loads, behind[at], beyond, outs
+        )
     return tuple(outs)
 
 

time: 77.4 us -> 84.3 us (1.089)
  the two profiles are of different devices: /device:TPU:1 before, /device:TPU:26 now
where the time goes in v1:
time: 84.3 us; the launch traced here: 84.1 us
  waiting for transfers between devices  41.3 us (49%)
  Pallas kernels  20.9 us (25%)
  starting transfers between devices  20.4 us (24%)
  between operations  1.29 us (2%)
    ppermute x7, waiting for transfers between devices, from_behind(): return lax.ppermute(block, axis, route)  22.6 us
    ppermute x7, starting transfers between devices, from_behind(): return lax.ppermute(block, axis, route)  18.9 us
    ppermute x1, waiting for transfers between devices, crossed(): lax.ppermute(block, 'lon', [(i, i ^ 1) for i in range(lax.axis_size('lon'...  17.5 us
    pallas_call x4, Pallas kernels, final(): pl.pallas_call(functools.partial(final_kernel, *spares, start), grid=(cou...  9.63 us
    pallas_call x4, Pallas kernels, pack(): pl.pallas_call(functools.partial(pack_kernel, *spares, start), grid=(coun...  6.9 us
    pallas_call x1, Pallas kernels, species_sums(): pl.pallas_call(species_kernel, out_shape=(jax.ShapeDtypeStruct((2, BINS,...  2.28 us
  transfers between devices with their start and end apart: 12, of which 5 were waited for; matrix products, arithmetic and copies ran while one was open for 0% of the time, Pallas kernels for 16%

profile of v1, /device:TPU:26, one launch (start us, length us, event | category | flops | bytes accessed | tf_op | source)
XLA Modules:
  0.0 84.1 jit_solution(7301741127012378080)
XLA Ops:
  0.6 1.4 %tables.1 = (s32[64,128]{1,0:T(8,128)S(1)}, s32[112,128]{1,0:T(8,128)S(1)}, s32[1]{0:T(128)}) custom-call(s32[1,128]{1,0:T(1,128)} %bitcast.5), custom_call_target="tpu_custom_call" | custom-call | tf_op jit(solution)/shard_map/tables/pallas_call | solution.py:125
  2.7 81.5 %conditional.1 = ((f32[10,9,4,16,128]{4,3,2,1,0:T(8,128)}, f32[10,4,16,128]{3,2,1,0:T(8,128)})) conditional(s32[]{:T(128)} %bitcast.4, (s32[]{:T(128)}, s32[1,128]{1,0:T(1,128)}, f32[10,9,4,16,128]{4,3,2,1,0:T(8,128)}, s32[64,128]{1,0:T(8,128)S(1)}, f32[1,16,128]{2,1,0:T(8,128)}, /*index=5*/f32[1,16,128]{2,1,0:T(8,128)}, ...), branch_computations={%region_0.1_spmd, %region_1.2_spmd, %region_2.3_spmd} | conditional | flops 224284 | bytes 47179560 | solution.py:709
  2.7 0.0 copy-start.12
  2.7 0.0 copy-start
  2.7 0.0 copy-start.6
  2.7 0.0 copy-start.15
  2.7 2.3 %species_sums.3 = (f32[2,9,16,128]{3,2,1,0:T(8,128)S(1)}, f32[2,9,16,128]{3,2,1,0:T(8,128)S(1)}) custom-call(s32[1]{0:T(128)} %bitcast.me_ref, s32[1,128]{1,0:T(1,128)} %get-tuple-element.48.shifts_ref, f32[10,9,4,16,128]{4,3,2,1,0:T(8,128)} %get-tuple-element.190.loads_ref, s32[64,128]{1,0:T(8,128)S(1)} %get-tuple-element.49.after_ref.near_ref), custom_call_target="tpu_custom_call" | custom-call | flops 1 | bytes 1 | tf_op jit(solution)/shard_map/cond/branch_0_fun/species_sums/pallas_call | solution.py:264
  5.0 0.1 collective-permute-start
  5.1 0.0 copy-done.12
  5.2 2.4 %collective-permute-start.1 = (f32[1,1,128]{2,1,0:T(1,128)S(1)}, f32[1,1,128]{2,1,0:T(1,128)S(1)}, u32[]{:S(2)}, u32[]{:S(2)}) collective-permute-start(f32[1,1,128]{2,1,0:T(1,128)S(1)} %slice.6), channel_id=1, source_target_pairs={{4,0},{8,4},{12,8},{16,12},{20,16},{24,20},{28,24},{32,28},{36,32}... | collective-permute-start | bytes 1544 | tf_op jit(solution)/shard_map/cond/branch_0_fun/ppermute | solution.py:30
  7.5 0.0 copy-done
  7.5 0.0 copy-done.6
  7.5 1.0 %pack_0.3 = (f32[2,328,128]{2,1,0:T(8,128)S(1)}, f32[10,72,128]{2,1,0:T(8,128)S(1)}) custom-call(s32[1,128]{1,0:T(1,128)S(1)} %copy-done.6, s32[64,128]{1,0:T(8,128)S(1)} %get-tuple-element.49.after_ref.near_ref, s32[112,128]{1,0:T(8,128)S(1)} %get-tuple-element.50.polar_ref, f32[10,9,4,16,128]{4,3,2,1,0:T(8,128)S(1)} %copy-done, ...), custom_call_target="tpu_custom_call" | custom-call | flops 1 | bytes 1 | tf_op jit(solution)/shard_map/cond/branch_0_fun/pack_0/pallas_call | solution.py:470
  8.6 1.7 %collective-permute-done.1.east_ref = f32[1,1,128]{2,1,0:T(1,128)S(1)} collective-permute-done((f32[1,1,128]{2,1,0:T(1,128)S(1)}, f32[1,1,128]{2,1,0:T(1,128)S(1)}, u32[]{:S(2)}, u32[]{:S(2)}) %collective-permute-start.1) | collective-permute-done | bytes 544 | tf_op jit(solution)/shard_map/cond/branch_0_fun/ppermute | solution.py:30
  10.3 0.0 collective-permute-done.got_ref
  10.3 0.0 copy-done.15
  10.3 1.5 %pack_7.3 = (f32[3,328,128]{2,1,0:T(8,128)S(1)}, f32[10,72,128]{2,1,0:T(8,128)S(1)}) custom-call(s32[1,128]{1,0:T(1,128)S(1)} %copy-done.6, s32[64,128]{1,0:T(8,128)S(1)} %get-tuple-element.49.after_ref.near_ref, s32[112,128]{1,0:T(8,128)S(1)} %get-tuple-element.50.polar_ref, f32[10,9,4,16,128]{4,3,2,1,0:T(8,128)S(1)} %copy-done, ...), custom_call_target="tpu_custom_call", output_to_operand_aliasing={{1}: (6, {})} | custom-call | flops 1 | bytes 1 | tf_op jit(solution)/shard_map/cond/branch_0_fun/pack_7/pallas_call | solution.py:470
  11.8 0.7 collective-permute-start.3
  12.5 0.6 collective-permute-start.2
  13.2 6.7 %collective-permute-start.6 = (f32[2,328,128]{2,1,0:T(8,128)S(1)}, f32[2,328,128]{2,1,0:T(8,128)S(1)}, u32[]{:S(2)}, u32[]{:S(2)}) collective-permute-start(f32[2,328,128]{2,1,0:T(8,128)S(1)} %get-tuple-element.69.rest_0_), channel_id=1, source_target_pairs={{252,0},{0,4},{4,8},{8,12},{12,16},{16,20},{20,24},{24,28},{28,32}... | collective-permute-start | bytes 1007624 | tf_op jit(solution)/shard_map/cond/branch_0_fun/ppermute | solution.py:30
  19.8 2.8 %pack_5.3 = (f32[2,328,128]{2,1,0:T(8,128)S(1)}, f32[10,72,128]{2,1,0:T(8,128)S(1)}) custom-call(s32[1,128]{1,0:T(1,128)S(1)} %copy-done.6, s32[64,128]{1,0:T(8,128)S(1)} %get-tuple-element.49.after_ref.near_ref, s32[112,128]{1,0:T(8,128)S(1)} %get-tuple-element.50.polar_ref, ...), custom_call_target="tpu_custom_call", output_to_operand_aliasing={{1}: (5, {})} | custom-call | flops 1 | bytes 1 | tf_op jit(solution)/shard_map/cond/branch_0_fun/pack_5/pallas_call | solution.py:470
  22.7 0.0 collective-permute-done.2.other_ref
  22.7 0.2 all_sums.3
  22.9 1.1 %collective-permute-start.5 = (f32[40,128]{1,0:T(8,128)S(1)}, f32[40,128]{1,0:T(8,128)S(1)}, u32[]{:S(2)}, u32[]{:S(2)}) collective-permute-start(f32[40,128]{1,0:T(8,128)S(1)} %get-tuple-element.62), channel_id=1, source_target_pairs={{248,0},{252,4},{0,8},{4,12},{8,16},{12,20},{16,24},{20,28},{24,32... | collective-permute-start | bytes 61448 | tf_op jit(solution)/shard_map/cond/branch_0_fun/ppermute | solution.py:30
  24.0 3.7 %collective-permute-start.4 = (f32[168,128]{1,0:T(8,128)S(1)}, f32[168,128]{1,0:T(8,128)S(1)}, u32[]{:S(2)}, u32[]{:S(2)}) collective-permute-start(f32[168,128]{1,0:T(8,128)S(1)} %get-tuple-element.61), channel_id=1, source_target_pairs={{252,0},{0,4},{4,8},{8,12},{12,16},{16,20},{20,24},{24,28},{28,32}... | collective-permute-start | bytes 258056 | tf_op jit(solution)/shard_map/cond/branch_0_fun/ppermute | solution.py:30
  27.7 0.0 copy-done.1
  27.7 1.5 %pack_2.3 = (f32[3,328,128]{2,1,0:T(8,128)S(1)}, f32[10,72,128]{2,1,0:T(8,128)S(1)}) custom-call(s32[1,128]{1,0:T(1,128)S(1)} %copy-done.6, s32[64,128]{1,0:T(8,128)S(1)} %get-tuple-element.49.after_ref.near_ref, s32[112,128]{1,0:T(8,128)S(1)} %get-tuple-element.50.polar_ref, f32[10,9,4,16,128]{4,3,2,1,0:T(8,128)S(1)} %copy-done.1, ...), custom_call_target="tpu_custom_call", output_to_operand_aliasing={{1}: (6, {})} | custom-call | flops 1 | bytes 1 | tf_op jit(solution)/shard_map/cond/branch_0_fun/pack_2/pallas_call | solution.py:470
  29.2 1.0 %collective-permute-start.11 = (f32[3,328,128]{2,1,0:T(8,128)S(1)}, f32[3,328,128]{2,1,0:T(8,128)S(1)}, u32[]{:S(2)}, u32[]{:S(2)}) collective-permute-start(f32[3,328,128]{2,1,0:T(8,128)S(1)} %get-tuple-element.68), channel_id=1, source_target_pairs={{252,0},{0,4},{4,8},{8,12},{12,16},{16,20},{20,24},{24,28},{28,32}... | collective-permute-start | bytes 1511432 | tf_op jit(solution)/shard_map/cond/branch_0_fun/ppermute | solution.py:30
  30.2 0.0 collective-permute-done.3
  30.2 0.1 broadcast_select_fusion
  30.2 13.6 %collective-permute-done.5.beyond_ref = f32[40,128]{1,0:T(8,128)S(1)} collective-permute-done((f32[40,128]{1,0:T(8,128)S(1)}, f32[40,128]{1,0:T(8,128)S(1)}, u32[]{:S(2)}, u32[]{:S(2)}) %collective-permute-start.5) | collective-permute-done | bytes 20512 | tf_op jit(solution)/shard_map/cond/branch_0_fun/ppermute | solution.py:30
  43.8 0.0 collective-permute-done.4.behind_ref
  43.8 0.0 collective-permute-start.10
  43.8 0.6 collective-permute-start.9
  44.4 0.0 collective-permute-done.6.after_ref.behind_ref
  44.4 3.5 %collective-permute-start.8 = (f32[2,328,128]{2,1,0:T(8,128)S(1)}, f32[2,328,128]{2,1,0:T(8,128)S(1)}, u32[]{:S(2)}, u32[]{:S(2)}) collective-permute-start(f32[2,328,128]{2,1,0:T(8,128)S(1)} %get-tuple-element.76.rest_0_), channel_id=1, source_target_pairs={{252,0},{0,4},{4,8},{8,12},{12,16},{16,20},{20,24},{24,28},{28,32}... | collective-permute-start | bytes 1007624 | tf_op jit(solution)/shard_map/cond/branch_0_fun/ppermute | solution.py:30
  48.0 0.3 organic.3.pair_ref
  48.3 0.1 collective-permute-start.7
  48.4 1.2 %collective-permute-done.7.other_ref = f32[2,48,128]{2,1,0:T(8,128)S(1)} collective-permute-done((f32[2,48,128]{2,1,0:T(8,128)S(1)}, f32[2,48,128]{2,1,0:T(8,128)S(1)}, u32[]{:S(2)}, u32[]{:S(2)}) %collective-permute-start.7) | collective-permute-done | bytes 49184 | tf_op jit(solution)/shard_map/cond/branch_0_fun/ppermute | solution.py:35
  49.6 0.1 weights.3
  49.7 7.3 %collective-permute-done.9.beyond_ref = f32[10,72,128]{2,1,0:T(8,128)S(1)} collective-permute-done((f32[10,72,128]{2,1,0:T(8,128)S(1)}, f32[10,72,128]{2,1,0:T(8,128)S(1)}, u32[]{:S(2)}, u32[]{:S(2)}) %collective-permute-start.9) | collective-permute-done | bytes 368672 | tf_op jit(solution)/shard_map/cond/branch_0_fun/ppermute | solution.py:30
  57.0 2.1 %final_0.3 = (f32[10,9,4,16,128]{4,3,2,1,0:T(8,128)}, f32[10,4,16,128]{3,2,1,0:T(8,128)}) custom-call(s32[1,128]{1,0:T(1,128)S(1)} %copy-done.6, s32[64,128]{1,0:T(8,128)S(1)} %get-tuple-element.49.after_ref.near_ref, s32[112,128]{1,0:T(8,128)S(1)} %get-tuple-element.50.polar_ref, f32[9,4,16,128]{3,2,1,0:T(8,128)S(1)} %get-tuple-element.72.near_w, ...), custom_call_target="tpu_custom_call" | custom-call | flops 1 | bytes 1 | tf_op jit(solution)/shard_map/cond/branch_0_fun/final_0/pallas_call | solution.py:638
  59.1 0.0 collective-permute-done.11.behind_ref
  59.1 2.8 %final_2.3 = (f32[10,9,4,16,128]{4,3,2,1,0:T(8,128)}, f32[10,4,16,128]{3,2,1,0:T(8,128)}) custom-call(s32[1,128]{1,0:T(1,128)S(1)} %copy-done.6, s32[64,128]{1,0:T(8,128)S(1)} %get-tuple-element.49.after_ref.near_ref, s32[112,128]{1,0:T(8,128)S(1)} %get-tuple-element.50.polar_ref, ...), custom_call_target="tpu_custom_call", output_to_operand_aliasing={{0}: (10, {}), {1}: (11, {})} | custom-call | flops 1 | bytes 1 | tf_op jit(solution)/shard_map/cond/branch_0_fun/final_2/pallas_call | solution.py:638
  61.8 17.5 %collective-permute-done.10.behind_ref = f32[3,328,128]{2,1,0:T(8,128)S(1)} collective-permute-done((f32[3,328,128]{2,1,0:T(8,128)S(1)}, f32[3,328,128]{2,1,0:T(8,128)S(1)}, u32[]{:S(2)}, u32[]{:S(2)}) %collective-permute-start.10) | collective-permute-done | bytes 503840 | tf_op jit(solution)/shard_map/cond/branch_0_fun/ppermute | solution.py:660
  79.3 2.7 %final_7.3 = (f32[10,9,4,16,128]{4,3,2,1,0:T(8,128)}, f32[10,4,16,128]{3,2,1,0:T(8,128)}) custom-call(s32[1,128]{1,0:T(1,128)S(1)} %copy-done.6, s32[64,128]{1,0:T(8,128)S(1)} %get-tuple-element.49.after_ref.near_ref, s32[112,128]{1,0:T(8,128)S(1)} %get-tuple-element.50.polar_ref, ...), custom_call_target="tpu_custom_call", output_to_operand_aliasing={{0}: (10, {}), {1}: (11, {})} | custom-call | flops 1 | bytes 1 | tf_op jit(solution)/shard_map/cond/branch_0_fun/final_7/pallas_call | solution.py:638
  82.1 0.0 collective-permute-done.8.behind_ref
  82.1 2.1 %final_5.3 = (f32[10,9,4,16,128]{4,3,2,1,0:T(8,128)}, f32[10,4,16,128]{3,2,1,0:T(8,128)}) custom-call(s32[1,128]{1,0:T(1,128)S(1)} %copy-done.6, s32[64,128]{1,0:T(8,128)S(1)} %get-tuple-element.49.after_ref.near_ref, s32[112,128]{1,0:T(8,128)S(1)} %get-tuple-element.50.polar_ref, ...), custom_call_target="tpu_custom_call", output_to_operand_aliasing={{0}: (10, {}), {1}: (11, {})} | custom-call | flops 1 | bytes 1 | tf_op jit(solution)/shard_map/cond/branch_0_fun/final_5/pallas_call | solution.py:638
  (5 shorter events, 0.0 us)
Async XLA Ops:
  2.7 2.4 %copy-start.12 = (f32[1,16,128]{2,1,0:T(8,128)S(1)}, f32[1,16,128]{2,1,0:T(8,128)}, u32[]{:S(2)}) copy-start(f32[1,16,128]{2,1,0:T(8,128)} %get-tuple-element.193.frac_ref) | copy-start | bytes 24580 | tf_op jit(solution)/shard_map/cond
  2.7 4.8 %copy-start = (f32[10,9,4,16,128]{4,3,2,1,0:T(8,128)S(1)}, f32[10,9,4,16,128]{4,3,2,1,0:T(8,128)}, u32[]{:S(2)}) copy-start(f32[10,9,4,16,128]{4,3,2,1,0:T(8,128)} %get-tuple-element.190.loads_ref) | copy-start | bytes 8847364 | tf_op jit(solution)/shard_map/cond
  2.7 4.8 %copy-start.6 = (s32[1,128]{1,0:T(1,128)S(1)}, s32[1,128]{1,0:T(1,128)}, u32[]{:S(2)}) copy-start(s32[1,128]{1,0:T(1,128)} %get-tuple-element.48.shifts_ref) | copy-start | bytes 1540 | tf_op jit(solution)/shard_map/cond
  2.7 7.6 %copy-start.15 = (f32[1,16,128]{2,1,0:T(8,128)S(1)}, f32[1,16,128]{2,1,0:T(8,128)}, u32[]{:S(2)}) copy-start(f32[1,16,128]{2,1,0:T(8,128)} %get-tuple-element.196.temp_ref) | copy-start | bytes 24580 | tf_op jit(solution)/shard_map/cond
  5.0 5.2 %collective-permute-start = (f32[2,9,16,128]{3,2,1,0:T(8,128)S(1)}, f32[2,9,16,128]{3,2,1,0:T(8,128)S(1)}, u32[]{:S(2)}, u32[]{:S(2)}) collective-permute-start(f32[2,9,16,128]{3,2,1,0:T(8,128)S(1)} %get-tuple-element.54), channel_id=1, source_target_pairs={{0,1},{1,0},{2,3},{3,2},{4,5},{5,4},{6,7},{7,6},{8,9},{9,8},{10,11... | collective-permute-start | bytes 442376 | tf_op jit(solution)/shard_map/cond/branch_0_fun/ppermute | solution.py:35
  5.2 5.1 %collective-permute-start.1 = (f32[1,1,128]{2,1,0:T(1,128)S(1)}, f32[1,1,128]{2,1,0:T(1,128)S(1)}, u32[]{:S(2)}, u32[]{:S(2)}) collective-permute-start(f32[1,1,128]{2,1,0:T(1,128)S(1)} %slice.6), channel_id=1, source_target_pairs={{4,0},{8,4},{12,8},{16,12},{20,16},{24,20},{28,24},{32,28},{36,32}... | collective-permute-start | bytes 1544 | tf_op jit(solution)/shard_map/cond/branch_0_fun/ppermute | solution.py:30
  11.8 18.3 %collective-permute-start.3 = (f32[3,328,128]{2,1,0:T(8,128)S(1)}, f32[3,328,128]{2,1,0:T(8,128)S(1)}, u32[]{:S(2)}, u32[]{:S(2)}) collective-permute-start(f32[3,328,128]{2,1,0:T(8,128)S(1)} %get-tuple-element.60.rest_0_), channel_id=1, source_target_pairs={{4,12},{12,20},{20,28},{28,36},{36,44},{44,52},{52,60},{60,68},{68... | collective-permute-start | bytes 1511432 | tf_op jit(solution)/shard_map/cond/branch_0_fun/ppermute | solution.py:656
  12.5 10.1 %collective-permute-start.2 = (f32[336,128]{1,0:T(8,128)S(1)}, f32[336,128]{1,0:T(8,128)S(1)}, u32[]{:S(2)}, u32[]{:S(2)}) collective-permute-start(f32[336,128]{1,0:T(8,128)S(1)} %chip_sums.3.mine_ref.rest_1_), channel_id=1, source_target_pairs={{0,2},{1,3},{2,0},{3,1},{4,6},{5,7},{6,4},{7,5},{8,10},{9,11},{10,... | collective-permute-start | bytes 516104 | tf_op jit(solution)/shard_map/cond/branch_0_fun/ppermute | solution.py:35
  13.2 14.5 %copy-start.1 = (f32[10,9,4,16,128]{4,3,2,1,0:T(8,128)S(1)}, f32[10,9,4,16,128]{4,3,2,1,0:T(8,128)}, u32[]{:S(2)}) copy-start(f32[10,9,4,16,128]{4,3,2,1,0:T(8,128)} %get-tuple-element.190.loads_ref) | copy-start | bytes 8847364 | tf_op jit(solution)/shard_map/cond
  13.2 31.3 %collective-permute-start.6 = (f32[2,328,128]{2,1,0:T(8,128)S(1)}, f32[2,328,128]{2,1,0:T(8,128)S(1)}, u32[]{:S(2)}, u32[]{:S(2)}) collective-permute-start(f32[2,328,128]{2,1,0:T(8,128)S(1)} %get-tuple-element.69.rest_0_), channel_id=1, source_target_pairs={{252,0},{0,4},{4,8},{8,12},{12,16},{16,20},{20,24},{24,28},{28,32}... | collective-permute-start | bytes 1007624 | tf_op jit(solution)/shard_map/cond/branch_0_fun/ppermute | solution.py:30
  22.9 20.9 %collective-permute-start.5 = (f32[40,128]{1,0:T(8,128)S(1)}, f32[40,128]{1,0:T(8,128)S(1)}, u32[]{:S(2)}, u32[]{:S(2)}) collective-permute-start(f32[40,128]{1,0:T(8,128)S(1)} %get-tuple-element.62), channel_id=1, source_target_pairs={{248,0},{252,4},{0,8},{4,12},{8,16},{12,20},{16,24},{20,28},{24,32... | collective-permute-start | bytes 61448 | tf_op jit(solution)/shard_map/cond/branch_0_fun/ppermute | solution.py:30
  24.0 19.8 %collective-permute-start.4 = (f32[168,128]{1,0:T(8,128)S(1)}, f32[168,128]{1,0:T(8,128)S(1)}, u32[]{:S(2)}, u32[]{:S(2)}) collective-permute-start(f32[168,128]{1,0:T(8,128)S(1)} %get-tuple-element.61), channel_id=1, source_target_pairs={{252,0},{0,4},{4,8},{8,12},{12,16},{16,20},{20,24},{24,28},{28,32}... | collective-permute-start | bytes 258056 | tf_op jit(solution)/shard_map/cond/branch_0_fun/ppermute | solution.py:30
  27.7 21.9 %copy-start.9 = (f32[3,16,128]{2,1,0:T(8,128)S(1)}, f32[3,16,128]{2,1,0:T(8,128)}, u32[]{:S(2)}) copy-start(f32[3,16,128]{2,1,0:T(8,128)} %get-tuple-element.199.diff_ref) | copy-start | bytes 73732 | tf_op jit(solution)/shard_map/cond
  29.2 29.9 %collective-permute-start.11 = (f32[3,328,128]{2,1,0:T(8,128)S(1)}, f32[3,328,128]{2,1,0:T(8,128)S(1)}, u32[]{:S(2)}, u32[]{:S(2)}) collective-permute-start(f32[3,328,128]{2,1,0:T(8,128)S(1)} %get-tuple-element.68), channel_id=1, source_target_pairs={{252,0},{0,4},{4,8},{8,12},{12,16},{16,20},{20,24},{24,28},{28,32}... | collective-permute-start | bytes 1511432 | tf_op jit(solution)/shard_map/cond/branch_0_fun/ppermute | solution.py:30
  43.8 35.5 %collective-permute-start.10 = (f32[3,328,128]{2,1,0:T(8,128)S(1)}, f32[3,328,128]{2,1,0:T(8,128)S(1)}, u32[]{:S(2)}, u32[]{:S(2)}) collective-permute-start(f32[3,328,128]{2,1,0:T(8,128)S(1)} %broadcast_select_fusion), channel_id=1, source_target_pairs={{0,4},{4,0},{8,12},{12,8},{16,20},{20,16},{24,28},{28,24},{32,36},... | collective-permute-start | bytes 1511432 | tf_op jit(solution)/shard_map/cond/branch_0_fun/ppermute | solution.py:660
  43.8 13.2 %collective-permute-start.9 = (f32[10,72,128]{2,1,0:T(8,128)S(1)}, f32[10,72,128]{2,1,0:T(8,128)S(1)}, u32[]{:S(2)}, u32[]{:S(2)}) collective-permute-start(f32[10,72,128]{2,1,0:T(8,128)S(1)} %get-tuple-element.77), channel_id=1, source_target_pairs={{248,0},{252,4},{0,8},{4,12},{8,16},{12,20},{16,24},{20,28},{24,32... | collective-permute-start | bytes 1105928 | tf_op jit(solution)/shard_map/cond/branch_0_fun/ppermute | solution.py:30
  44.4 37.6 %collective-permute-start.8 = (f32[2,328,128]{2,1,0:T(8,128)S(1)}, f32[2,328,128]{2,1,0:T(8,128)S(1)}, u32[]{:S(2)}, u32[]{:S(2)}) collective-permute-start(f32[2,328,128]{2,1,0:T(8,128)S(1)} %get-tuple-element.76.rest_0_), channel_id=1, source_target_pairs={{252,0},{0,4},{4,8},{8,12},{12,16},{16,20},{20,24},{24,28},{28,32}... | collective-permute-start | bytes 1007624 | tf_op jit(solution)/shard_map/cond/branch_0_fun/ppermute | solution.py:30
  48.3 1.3 %collective-permute-start.7 = (f32[2,48,128]{2,1,0:T(8,128)S(1)}, f32[2,48,128]{2,1,0:T(8,128)S(1)}, u32[]{:S(2)}, u32[]{:S(2)}) collective-permute-start(f32[2,48,128]{2,1,0:T(8,128)S(1)} %organic.3.pair_ref), channel_id=1, source_target_pairs={{0,1},{1,0},{2,3},{3,2},{4,5},{5,4},{6,7},{7,6},{8,9},{9,8},{10,11... | collective-permute-start | bytes 147464 | tf_op jit(solution)/shard_map/cond/branch_0_fun/ppermute | solution.py:35

commit v2 on v0

--- a/solution.py
+++ b/solution.py
@@ -670,18 +670,20 @@
     got = swapped(send, 1)
     mine = chip_sums(keep, got, frac, east, temp)
     other = swapped(mine, 2)
-    own, ahead_sums, beyond_sums = all_sums(spares, near_table, polar_table, mine, other)
     after, beyond, aheads = [keep], None, [None] * len(CHUNKS)
     for at in (0, last, 2, 1):
         aheads[at], beyond = pack(
             spares, starts[at], CHUNKS[at], *tables, loads, after, beyond
         )
-        after = [aheads[at], own] if at == 2 else [aheads[at]]
+        after = [aheads[at]]
+    other, aheads[1], beyond = lax.optimization_barrier((other, aheads[1], beyond))
+    own, ahead_sums, beyond_sums = all_sums(spares, near_table, polar_table, mine, other)
     relayed = along_meridian(aheads[last])
     aheads[0], _ = lax.optimization_barrier((aheads[0], mine))
-    behind = [from_behind(aheads[0], "lon", 1), from_behind(aheads[1], "lon", 1)]
     sums_behind = from_behind(ahead_sums, "lon", 1)
     sums_beyond = from_behind(beyond_sums, "lon", 2)
+    aheads[1], sums_beyond = lax.optimization_barrier((aheads[1], sums_beyond))
+    behind = [from_behind(aheads[0], "lon", 1), from_behind(aheads[1], "lon", 1)]
     beyond = from_behind(beyond, "lon", 2)
     aheads[2], behind[0] = lax.optimization_barrier((aheads[2], behind[0]))
     behind.append(from_behind(aheads[2], "lon", 1))

time: 77.4 us -> 76.6 us (0.990)
  starting transfers between devices: 22.7 us -> 20.7 us
  waiting for transfers between devices: 32 us -> 33.3 us
    ppermute x7, waiting for transfers between devices: 23 us -> 26.6 us  [from_behind(): return lax.ppermute(block, axis, route)]
    ppermute x7, starting transfers between devices: 15.2 us -> 12 us  [from_behind(): return lax.ppermute(block, axis, route)]
    ppermute x3, waiting for transfers between devices: 8.91 us -> 6.74 us  [swapped(): return lax.ppermute(block, 'spc', route)]
    pallas_call x4, Pallas kernels: 7.07 us -> 5.09 us  [pack(): pl.pallas_call(functools.partial(pack_kernel, *spares, start), grid=(coun...]
    pallas_call x4, Pallas kernels: 9.63 us -> 11.4 us  [final(): pl.pallas_call(functools.partial(final_kernel, *spares, start), grid=(cou...]
  transfers between devices with their start and end apart: 12 -> 12, of which waited for: 6 -> 7; matrix products, arithmetic and copies ran while one was open for 0% -> 0% of each run, Pallas kernels for 20% -> 20%
where the time goes in v2:
time: 76.6 us; the launch traced here: 76.4 us
  waiting for transfers between devices  33.3 us (43%)
  Pallas kernels  20.9 us (27%)
  starting transfers between devices  20.7 us (27%)
  between operations  1.29 us (2%)
    ppermute x7, waiting for transfers between devices, from_behind(): return lax.ppermute(block, axis, route)  26.6 us
    ppermute x7, starting transfers between devices, from_behind(): return lax.ppermute(block, axis, route)  12 us
    pallas_call x4, Pallas kernels, final(): pl.pallas_call(functools.partial(final_kernel, *spares, start), grid=(cou...  11.4 us
    ppermute x3, starting transfers between devices, swapped(): return lax.ppermute(block, 'spc', route)  7.27 us
    ppermute x3, waiting for transfers between devices, swapped(): return lax.ppermute(block, 'spc', route)  6.74 us
    pallas_call x4, Pallas kernels, pack(): pl.pallas_call(functools.partial(pack_kernel, *spares, start), grid=(coun...  5.09 us
    pallas_call x1, Pallas kernels, species_sums(): pl.pallas_call(species_kernel, out_shape=(jax.ShapeDtypeStruct((2, BINS,...  2.28 us
  transfers between devices with their start and end apart: 12, of which 7 were waited for; matrix products, arithmetic and copies ran while one was open for 0% of the time, Pallas kernels for 20%

profile of v2, /device:TPU:1, one launch (start us, length us, event | category | flops | bytes accessed | tf_op | source)
XLA Modules:
  0.0 76.4 jit_solution(10317215007279670821)
XLA Ops:
  0.6 1.4 %tables.1 = (s32[64,128]{1,0:T(8,128)S(1)}, s32[112,128]{1,0:T(8,128)S(1)}, s32[1]{0:T(128)}) custom-call(s32[1,128]{1,0:T(1,128)} %bitcast.5), custom_call_target="tpu_custom_call" | custom-call | tf_op jit(solution)/shard_map/tables/pallas_call | solution.py:125
  2.7 73.7 %conditional.1 = ((f32[10,9,4,16,128]{4,3,2,1,0:T(8,128)}, f32[10,4,16,128]{3,2,1,0:T(8,128)})) conditional(s32[]{:T(128)} %bitcast.4, (s32[]{:T(128)}, s32[1,128]{1,0:T(1,128)}, f32[10,9,4,16,128]{4,3,2,1,0:T(8,128)}, s32[64,128]{1,0:T(8,128)S(1)}, f32[1,16,128]{2,1,0:T(8,128)}, /*index=5*/f32[1,16,128]{2,1,0:T(8,128)}, ...), branch_computations={%region_0.1_spmd, %region_1.2_spmd, %region_2.3_spmd} | conditional | flops 149532 | bytes 45545308 | solution.py:707
  2.7 0.0 copy-start.14
  2.7 0.0 copy-start
  2.7 0.0 copy-start.8
  2.7 0.0 copy-start.17
  2.7 2.3 %species_sums.3 = (f32[2,9,16,128]{3,2,1,0:T(8,128)S(1)}, f32[2,9,16,128]{3,2,1,0:T(8,128)S(1)}) custom-call(s32[1]{0:T(128)} %bitcast.me_ref, s32[1,128]{1,0:T(1,128)} %get-tuple-element.48.shifts_ref, f32[10,9,4,16,128]{4,3,2,1,0:T(8,128)} %get-tuple-element.205.loads_ref, s32[64,128]{1,0:T(8,128)S(1)} %get-tuple-element.49.after_ref.near_ref), custom_call_target="tpu_custom_call" | custom-call | flops 1 | bytes 1 | tf_op jit(solution)/shard_map/cond/branch_0_fun/species_sums/pallas_call | solution.py:264
  5.0 3.3 %collective-permute-start = (f32[2,9,16,128]{3,2,1,0:T(8,128)S(1)}, f32[2,9,16,128]{3,2,1,0:T(8,128)S(1)}, u32[]{:S(2)}, u32[]{:S(2)}) collective-permute-start(f32[2,9,16,128]{3,2,1,0:T(8,128)S(1)} %get-tuple-element.54), channel_id=1, source_target_pairs={{0,1},{1,0},{2,3},{3,2},{4,5},{5,4},{6,7},{7,6},{8,9},{9,8},{10,11... | collective-permute-start | bytes 442376 | tf_op jit(solution)/shard_map/cond/branch_0_fun/ppermute | solution.py:35
  8.4 0.0 copy-done.14
  8.4 8.8 %collective-permute-start.1 = (f32[1,1,128]{2,1,0:T(1,128)S(1)}, f32[1,1,128]{2,1,0:T(1,128)S(1)}, u32[]{:S(2)}, u32[]{:S(2)}) collective-permute-start(f32[1,1,128]{2,1,0:T(1,128)S(1)} %slice.6), channel_id=1, source_target_pairs={{4,0},{8,4},{12,8},{16,12},{20,16},{24,20},{28,24},{32,28},{36,32}... | collective-permute-start | bytes 1544 | tf_op jit(solution)/shard_map/cond/branch_0_fun/ppermute | solution.py:30
  17.1 0.0 copy-done
  17.1 0.0 copy-done.8
  17.2 1.0 %pack_0.3 = (f32[2,328,128]{2,1,0:T(8,128)S(1)}, f32[10,72,128]{2,1,0:T(8,128)S(1)}) custom-call(s32[1,128]{1,0:T(1,128)S(1)} %copy-done.8, s32[64,128]{1,0:T(8,128)S(1)} %get-tuple-element.49.after_ref.near_ref, s32[112,128]{1,0:T(8,128)S(1)} %get-tuple-element.50.polar_ref, f32[10,9,4,16,128]{4,3,2,1,0:T(8,128)S(1)} %copy-done, ...), custom_call_target="tpu_custom_call" | custom-call | flops 1 | bytes 1 | tf_op jit(solution)/shard_map/cond/branch_0_fun/pack_0/pallas_call | solution.py:470
  18.2 0.0 collective-permute-done.1.east_ref
  18.2 0.0 collective-permute-done.got_ref
  18.2 0.1 collective-permute-start.6
  18.3 1.0 %pack_8.3 = (f32[2,328,128]{2,1,0:T(8,128)S(1)}, f32[10,72,128]{2,1,0:T(8,128)S(1)}) custom-call(s32[1,128]{1,0:T(1,128)S(1)} %copy-done.8, s32[64,128]{1,0:T(8,128)S(1)} %get-tuple-element.49.after_ref.near_ref, s32[112,128]{1,0:T(8,128)S(1)} %get-tuple-element.50.polar_ref, f32[10,9,4,16,128]{4,3,2,1,0:T(8,128)S(1)} %copy-done, ...), custom_call_target="tpu_custom_call", output_to_operand_aliasing={{1}: (5, {})} | custom-call | flops 1 | bytes 1 | tf_op jit(solution)/shard_map/cond/branch_0_fun/pack_8/pallas_call | solution.py:470
  19.3 1.4 %collective-permute-start.3 = (f32[2,328,128]{2,1,0:T(8,128)S(1)}, f32[2,328,128]{2,1,0:T(8,128)}, u32[]{:S(2)}, u32[]{:S(2)}) collective-permute-start(f32[2,328,128]{2,1,0:T(8,128)S(1)} %get-tuple-element.59.rest_0_), channel_id=1, source_target_pairs={{4,12},{12,20},{20,28},{28,36},{36,44},{44,52},{52,60},{60,68},{68... | collective-permute-start | bytes 1007624 | tf_op jit(solution)/shard_map/cond/branch_0_fun/ppermute | solution.py:656
  20.8 0.3 collective-permute-start.2
  21.1 1.5 %pack_5.3 = (f32[3,328,128]{2,1,0:T(8,128)S(1)}, f32[10,72,128]{2,1,0:T(8,128)S(1)}) custom-call(s32[1,128]{1,0:T(1,128)S(1)} %copy-done.8, s32[64,128]{1,0:T(8,128)S(1)} %get-tuple-element.49.after_ref.near_ref, s32[112,128]{1,0:T(8,128)S(1)} %get-tuple-element.50.polar_ref, f32[10,9,4,16,128]{4,3,2,1,0:T(8,128)S(1)} %copy-done, ...), custom_call_target="tpu_custom_call", output_to_operand_aliasing={{1}: (5, {})} | custom-call | flops 1 | bytes 1 | tf_op jit(solution)/shard_map/cond/branch_0_fun/pack_5/pallas_call | solution.py:470
  22.6 0.0 copy-start.11
  22.6 1.5 %pack_2.3 = (f32[3,328,128]{2,1,0:T(8,128)S(1)}, f32[10,72,128]{2,1,0:T(8,128)S(1)}) custom-call(s32[1,128]{1,0:T(1,128)S(1)} %copy-done.8, s32[64,128]{1,0:T(8,128)S(1)} %get-tuple-element.49.after_ref.near_ref, s32[112,128]{1,0:T(8,128)S(1)} %get-tuple-element.50.polar_ref, f32[10,9,4,16,128]{4,3,2,1,0:T(8,128)S(1)} %copy-done, ...), custom_call_target="tpu_custom_call", output_to_operand_aliasing={{1}: (5, {})} | custom-call | flops 1 | bytes 1 | tf_op jit(solution)/shard_map/cond/branch_0_fun/pack_2/pallas_call | solution.py:470
  24.1 5.9 %collective-permute-done.2.other_ref = f32[336,128]{1,0:T(8,128)S(1)} collective-permute-done((f32[336,128]{1,0:T(8,128)S(1)}, f32[336,128]{1,0:T(8,128)S(1)}, u32[]{:S(2)}, u32[]{:S(2)}) %collective-permute-start.2) | collective-permute-done | bytes 172064 | tf_op jit(solution)/shard_map/cond/branch_0_fun/ppermute | solution.py:35
  30.0 0.2 all_sums.3
  30.2 0.1 collective-permute-start.5
  30.3 0.1 collective-permute-start.4
  30.4 0.1 collective-permute-start.9
  30.5 7.3 %collective-permute-done.5.beyond_ref = f32[40,128]{1,0:T(8,128)S(1)} collective-permute-done((f32[40,128]{1,0:T(8,128)S(1)}, f32[40,128]{1,0:T(8,128)S(1)}, u32[]{:S(2)}, u32[]{:S(2)}) %collective-permute-start.5) | collective-permute-done | bytes 20512 | tf_op jit(solution)/shard_map/cond/branch_0_fun/ppermute | solution.py:30
  37.8 2.9 %collective-permute-start.11 = (f32[3,328,128]{2,1,0:T(8,128)S(1)}, f32[3,328,128]{2,1,0:T(8,128)S(1)}, u32[]{:S(2)}, u32[]{:S(2)}) collective-permute-start(f32[3,328,128]{2,1,0:T(8,128)S(1)} %get-tuple-element.83), channel_id=1, source_target_pairs={{252,0},{0,4},{4,8},{8,12},{12,16},{16,20},{20,24},{24,28},{28,32}... | collective-permute-start | bytes 1511432 | tf_op jit(solution)/shard_map/cond/branch_0_fun/ppermute | solution.py:30
  40.7 0.0 collective-permute-done.6.after_ref.behind_ref
  40.7 0.0 collective-permute-start.10
  40.7 0.0 collective-permute-done.3
  40.7 0.0 copy-start.1
  40.8 2.0 %collective-permute-done.4.behind_ref = f32[168,128]{1,0:T(8,128)S(1)} collective-permute-done((f32[168,128]{1,0:T(8,128)S(1)}, f32[168,128]{1,0:T(8,128)S(1)}, u32[]{:S(2)}, u32[]{:S(2)}) %collective-permute-start.4) | collective-permute-done | bytes 86048 | tf_op jit(solution)/shard_map/cond/branch_0_fun/ppermute | solution.py:30
  42.7 0.0 collective-permute-start.8
  42.7 0.3 organic.3.pair_ref
  43.1 3.6 %collective-permute-start.7 = (f32[2,48,128]{2,1,0:T(8,128)S(1)}, f32[2,48,128]{2,1,0:T(8,128)S(1)}, u32[]{:S(2)}, u32[]{:S(2)}) collective-permute-start(f32[2,48,128]{2,1,0:T(8,128)S(1)} %organic.3.pair_ref), channel_id=1, source_target_pairs={{0,1},{1,0},{2,3},{3,2},{4,5},{5,4},{6,7},{7,6},{8,9},{9,8},{10,11... | collective-permute-start | bytes 147464 | tf_op jit(solution)/shard_map/cond/branch_0_fun/ppermute | solution.py:35
  46.7 0.9 %collective-permute-done.7.other_ref = f32[2,48,128]{2,1,0:T(8,128)S(1)} collective-permute-done((f32[2,48,128]{2,1,0:T(8,128)S(1)}, f32[2,48,128]{2,1,0:T(8,128)S(1)}, u32[]{:S(2)}, u32[]{:S(2)}) %collective-permute-start.7) | collective-permute-done | bytes 49184 | tf_op jit(solution)/shard_map/cond/branch_0_fun/ppermute | solution.py:35
  47.6 0.1 weights.3
  47.7 1.3 %collective-permute-done.9.beyond_ref = f32[10,72,128]{2,1,0:T(8,128)S(1)} collective-permute-done((f32[10,72,128]{2,1,0:T(8,128)S(1)}, f32[10,72,128]{2,1,0:T(8,128)S(1)}, u32[]{:S(2)}, u32[]{:S(2)}) %collective-permute-start.9) | collective-permute-done | bytes 368672 | tf_op jit(solution)/shard_map/cond/branch_0_fun/ppermute | solution.py:30
  49.0 3.9 %final_0.3 = (f32[10,9,4,16,128]{4,3,2,1,0:T(8,128)}, f32[10,4,16,128]{3,2,1,0:T(8,128)}) custom-call(s32[1,128]{1,0:T(1,128)S(1)} %copy-done.8, s32[64,128]{1,0:T(8,128)S(1)} %get-tuple-element.49.after_ref.near_ref, s32[112,128]{1,0:T(8,128)S(1)} %get-tuple-element.50.polar_ref, f32[9,4,16,128]{3,2,1,0:T(8,128)S(1)} %get-tuple-element.76.near_w, ...), custom_call_target="tpu_custom_call" | custom-call | flops 1 | bytes 1 | tf_op jit(solution)/shard_map/cond/branch_0_fun/final_0/pallas_call | solution.py:638
  52.9 8.0 %collective-permute-done.11.behind_ref = f32[3,328,128]{2,1,0:T(8,128)S(1)} collective-permute-done((f32[3,328,128]{2,1,0:T(8,128)S(1)}, f32[3,328,128]{2,1,0:T(8,128)S(1)}, u32[]{:S(2)}, u32[]{:S(2)}) %collective-permute-start.11) | collective-permute-done | bytes 503840 | tf_op jit(solution)/shard_map/cond/branch_0_fun/ppermute | solution.py:30
  60.8 0.0 copy-done.1
  60.8 2.7 %final_2.3 = (f32[10,9,4,16,128]{4,3,2,1,0:T(8,128)}, f32[10,4,16,128]{3,2,1,0:T(8,128)}) custom-call(s32[1,128]{1,0:T(1,128)S(1)} %copy-done.8, s32[64,128]{1,0:T(8,128)S(1)} %get-tuple-element.49.after_ref.near_ref, s32[112,128]{1,0:T(8,128)S(1)} %get-tuple-element.50.polar_ref, ...), custom_call_target="tpu_custom_call", output_to_operand_aliasing={{0}: (10, {}), {1}: (11, {})} | custom-call | flops 1 | bytes 1 | tf_op jit(solution)/shard_map/cond/branch_0_fun/final_2/pallas_call | solution.py:638
  63.6 8.1 %collective-permute-done.10.behind_ref = f32[3,328,128]{2,1,0:T(8,128)S(1)} collective-permute-done((f32[3,328,128]{2,1,0:T(8,128)S(1)}, f32[3,328,128]{2,1,0:T(8,128)S(1)}, u32[]{:S(2)}, u32[]{:S(2)}) %collective-permute-start.10) | collective-permute-done | bytes 503840 | tf_op jit(solution)/shard_map/cond/branch_0_fun/ppermute | solution.py:30
  71.6 2.7 %final_5.3 = (f32[10,9,4,16,128]{4,3,2,1,0:T(8,128)}, f32[10,4,16,128]{3,2,1,0:T(8,128)}) custom-call(s32[1,128]{1,0:T(1,128)S(1)} %copy-done.8, s32[64,128]{1,0:T(8,128)S(1)} %get-tuple-element.49.after_ref.near_ref, s32[112,128]{1,0:T(8,128)S(1)} %get-tuple-element.50.polar_ref, ...), custom_call_target="tpu_custom_call", output_to_operand_aliasing={{0}: (10, {}), {1}: (11, {})} | custom-call | flops 1 | bytes 1 | tf_op jit(solution)/shard_map/cond/branch_0_fun/final_5/pallas_call | solution.py:638
  74.3 0.0 collective-permute-done.8.behind_ref
  74.4 2.1 %final_8.3 = (f32[10,9,4,16,128]{4,3,2,1,0:T(8,128)}, f32[10,4,16,128]{3,2,1,0:T(8,128)}) custom-call(s32[1,128]{1,0:T(1,128)S(1)} %copy-done.8, s32[64,128]{1,0:T(8,128)S(1)} %get-tuple-element.49.after_ref.near_ref, s32[112,128]{1,0:T(8,128)S(1)} %get-tuple-element.50.polar_ref, ...), custom_call_target="tpu_custom_call", output_to_operand_aliasing={{0}: (10, {}), {1}: (11, {})} | custom-call | flops 1 | bytes 1 | tf_op jit(solution)/shard_map/cond/branch_0_fun/final_8/pallas_call | solution.py:638
  (5 shorter events, 0.1 us)
Async XLA Ops:
  2.7 5.7 %copy-start.14 = (f32[1,16,128]{2,1,0:T(8,128)S(1)}, f32[1,16,128]{2,1,0:T(8,128)}, u32[]{:S(2)}) copy-start(f32[1,16,128]{2,1,0:T(8,128)} %get-tuple-element.208.frac_ref) | copy-start | bytes 24580 | tf_op jit(solution)/shard_map/cond
  2.7 14.4 %copy-start = (f32[10,9,4,16,128]{4,3,2,1,0:T(8,128)S(1)}, f32[10,9,4,16,128]{4,3,2,1,0:T(8,128)}, u32[]{:S(2)}) copy-start(f32[10,9,4,16,128]{4,3,2,1,0:T(8,128)} %get-tuple-element.205.loads_ref) | copy-start | bytes 8847364 | tf_op jit(solution)/shard_map/cond
  2.7 14.4 %copy-start.8 = (s32[1,128]{1,0:T(1,128)S(1)}, s32[1,128]{1,0:T(1,128)}, u32[]{:S(2)}) copy-start(s32[1,128]{1,0:T(1,128)} %get-tuple-element.48.shifts_ref) | copy-start | bytes 1540 | tf_op jit(solution)/shard_map/cond
  2.7 15.5 %copy-start.17 = (f32[1,16,128]{2,1,0:T(8,128)S(1)}, f32[1,16,128]{2,1,0:T(8,128)}, u32[]{:S(2)}) copy-start(f32[1,16,128]{2,1,0:T(8,128)} %get-tuple-element.211.temp_ref) | copy-start | bytes 24580 | tf_op jit(solution)/shard_map/cond
  5.0 13.1 %collective-permute-start = (f32[2,9,16,128]{3,2,1,0:T(8,128)S(1)}, f32[2,9,16,128]{3,2,1,0:T(8,128)S(1)}, u32[]{:S(2)}, u32[]{:S(2)}) collective-permute-start(f32[2,9,16,128]{3,2,1,0:T(8,128)S(1)} %get-tuple-element.54), channel_id=1, source_target_pairs={{0,1},{1,0},{2,3},{3,2},{4,5},{5,4},{6,7},{7,6},{8,9},{9,8},{10,11... | collective-permute-start | bytes 442376 | tf_op jit(solution)/shard_map/cond/branch_0_fun/ppermute | solution.py:35
  8.4 9.8 %collective-permute-start.1 = (f32[1,1,128]{2,1,0:T(1,128)S(1)}, f32[1,1,128]{2,1,0:T(1,128)S(1)}, u32[]{:S(2)}, u32[]{:S(2)}) collective-permute-start(f32[1,1,128]{2,1,0:T(1,128)S(1)} %slice.6), channel_id=1, source_target_pairs={{4,0},{8,4},{12,8},{16,12},{20,16},{24,20},{28,24},{32,28},{36,32}... | collective-permute-start | bytes 1544 | tf_op jit(solution)/shard_map/cond/branch_0_fun/ppermute | solution.py:30
  18.2 22.4 %collective-permute-start.6 = (f32[2,328,128]{2,1,0:T(8,128)S(1)}, f32[2,328,128]{2,1,0:T(8,128)S(1)}, u32[]{:S(2)}, u32[]{:S(2)}) collective-permute-start(f32[2,328,128]{2,1,0:T(8,128)S(1)} %get-tuple-element.73.rest_0_), channel_id=1, source_target_pairs={{252,0},{0,4},{4,8},{8,12},{12,16},{16,20},{20,24},{24,28},{28,32}... | collective-permute-start | bytes 1007624 | tf_op jit(solution)/shard_map/cond/branch_0_fun/ppermute | solution.py:30
  19.3 21.4 %collective-permute-start.3 = (f32[2,328,128]{2,1,0:T(8,128)S(1)}, f32[2,328,128]{2,1,0:T(8,128)}, u32[]{:S(2)}, u32[]{:S(2)}) collective-permute-start(f32[2,328,128]{2,1,0:T(8,128)S(1)} %get-tuple-element.59.rest_0_), channel_id=1, source_target_pairs={{4,12},{12,20},{20,28},{28,36},{36,44},{44,52},{52,60},{60,68},{68... | collective-permute-start | bytes 1007624 | tf_op jit(solution)/shard_map/cond/branch_0_fun/ppermute | solution.py:656
  20.8 9.2 %collective-permute-start.2 = (f32[336,128]{1,0:T(8,128)S(1)}, f32[336,128]{1,0:T(8,128)S(1)}, u32[]{:S(2)}, u32[]{:S(2)}) collective-permute-start(f32[336,128]{1,0:T(8,128)S(1)} %chip_sums.3.mine_ref), channel_id=1, source_target_pairs={{0,2},{1,3},{2,0},{3,1},{4,6},{5,7},{6,4},{7,5},{8,10},{9,11},{10,... | collective-permute-start | bytes 516104 | tf_op jit(solution)/shard_map/cond/branch_0_fun/ppermute | solution.py:35
  22.6 25.0 %copy-start.11 = (f32[3,16,128]{2,1,0:T(8,128)S(1)}, f32[3,16,128]{2,1,0:T(8,128)}, u32[]{:S(2)}) copy-start(f32[3,16,128]{2,1,0:T(8,128)} %get-tuple-element.214.diff_ref) | copy-start | bytes 73732 | tf_op jit(solution)/shard_map/cond
  30.2 7.6 %collective-permute-start.5 = (f32[40,128]{1,0:T(8,128)S(1)}, f32[40,128]{1,0:T(8,128)S(1)}, u32[]{:S(2)}, u32[]{:S(2)}) collective-permute-start(f32[40,128]{1,0:T(8,128)S(1)} %get-tuple-element.69), channel_id=1, source_target_pairs={{248,0},{252,4},{0,8},{4,12},{8,16},{12,20},{16,24},{20,28},{24,32... | collective-permute-start | bytes 61448 | tf_op jit(solution)/shard_map/cond/branch_0_fun/ppermute | solution.py:30
  30.3 12.4 %collective-permute-start.4 = (f32[168,128]{1,0:T(8,128)S(1)}, f32[168,128]{1,0:T(8,128)S(1)}, u32[]{:S(2)}, u32[]{:S(2)}) collective-permute-start(f32[168,128]{1,0:T(8,128)S(1)} %get-tuple-element.67), channel_id=1, source_target_pairs={{252,0},{0,4},{4,8},{8,12},{12,16},{16,20},{20,24},{24,28},{28,32}... | collective-permute-start | bytes 258056 | tf_op jit(solution)/shard_map/cond/branch_0_fun/ppermute | solution.py:30
  30.4 18.5 %collective-permute-start.9 = (f32[10,72,128]{2,1,0:T(8,128)S(1)}, f32[10,72,128]{2,1,0:T(8,128)S(1)}, u32[]{:S(2)}, u32[]{:S(2)}) collective-permute-start(f32[10,72,128]{2,1,0:T(8,128)S(1)} %get-tuple-element.81), channel_id=1, source_target_pairs={{248,0},{252,4},{0,8},{4,12},{8,16},{12,20},{16,24},{20,28},{24,32... | collective-permute-start | bytes 1105928 | tf_op jit(solution)/shard_map/cond/branch_0_fun/ppermute | solution.py:30
  37.8 23.0 %collective-permute-start.11 = (f32[3,328,128]{2,1,0:T(8,128)S(1)}, f32[3,328,128]{2,1,0:T(8,128)S(1)}, u32[]{:S(2)}, u32[]{:S(2)}) collective-permute-start(f32[3,328,128]{2,1,0:T(8,128)S(1)} %get-tuple-element.83), channel_id=1, source_target_pairs={{252,0},{0,4},{4,8},{8,12},{12,16},{16,20},{20,24},{24,28},{28,32}... | collective-permute-start | bytes 1511432 | tf_op jit(solution)/shard_map/cond/branch_0_fun/ppermute | solution.py:30
  40.7 30.9 %collective-permute-start.10 = (f32[3,328,128]{2,1,0:T(8,128)S(1)}, f32[3,328,128]{2,1,0:T(8,128)S(1)}, u32[]{:S(2)}, u32[]{:S(2)}) collective-permute-start(f32[3,328,128]{2,1,0:T(8,128)S(1)} %get-tuple-element.82.rest_0_), channel_id=1, source_target_pairs={{252,0},{0,4},{4,8},{8,12},{12,16},{16,20},{20,24},{24,28},{28,32}... | collective-permute-start | bytes 1511432 | tf_op jit(solution)/shard_map/cond/branch_0_fun/ppermute | solution.py:30
  40.7 20.1 %copy-start.1 = (f32[10,9,4,16,128]{4,3,2,1,0:T(8,128)S(1)}, f32[10,9,4,16,128]{4,3,2,1,0:T(8,128)}, u32[]{:S(2)}) copy-start(f32[10,9,4,16,128]{4,3,2,1,0:T(8,128)} %get-tuple-element.205.loads_ref) | copy-start | bytes 8847364 | tf_op jit(solution)/shard_map/cond
  42.7 31.6 %collective-permute-start.8 = (f32[2,328,128]{2,1,0:T(8,128)S(1)}, f32[2,328,128]{2,1,0:T(8,128)S(1)}, u32[]{:S(2)}, u32[]{:S(2)}) collective-permute-start(f32[2,328,128]{2,1,0:T(8,128)S(1)} %broadcast_select_fusion), channel_id=1, source_target_pairs={{0,4},{4,0},{8,12},{12,8},{16,20},{20,16},{24,28},{28,24},{32,36},... | collective-permute-start | bytes 1007624 | tf_op jit(solution)/shard_map/cond/branch_0_fun/ppermute | solution.py:660
  43.1 4.5 %collective-permute-start.7 = (f32[2,48,128]{2,1,0:T(8,128)S(1)}, f32[2,48,128]{2,1,0:T(8,128)S(1)}, u32[]{:S(2)}, u32[]{:S(2)}) collective-permute-start(f32[2,48,128]{2,1,0:T(8,128)S(1)} %organic.3.pair_ref), channel_id=1, source_target_pairs={{0,1},{1,0},{2,3},{3,2},{4,5},{5,4},{6,7},{7,6},{8,9},{9,8},{10,11... | collective-permute-start | bytes 147464 | tf_op jit(solution)/shard_map/cond/branch_0_fun/ppermute | solution.py:35
